TPU v7x, 256 devices: a whole 4x4x8 slice. The times are simulated.
256 devices in a mesh: gx: 16 (over y_hi, x, core), gz: 8 (over z), gy: 2 (over y_lo).
Axes of the slice: x: 4, y: 4 (y_hi: 2, y_lo: 2; y = y_hi * 2 + y_lo), z: 8, core: 2. Of those that a mesh axis runs over, the one named last changes fastest.
Arguments:
- object_slab: float32 [2, 2, 2048, 1024], P(None, 'gy', 'gx', 'gz'), may hold values from -6 to 6
- depth_hops: int32 [16, 2, 1024], P(None, None, 'gz'), may hold values from -256 to 256, as said below
- depth_taps: float32 [16, 2, 8, 1024], P(None, None, None, 'gz'), may hold values from -2 to 2
- column_hops: int32 [16, 2048], P(None, 'gx'), may hold values from -128 to 128, as said below
- column_taps: float32 [16, 8, 2048], P(None, None, 'gx'), may hold values from -2 to 2
- angle_index: int32 [16], replicated, may hold values from 0 to 15, each once
- illumination: float32 [2, 2, 2048], P(None, 'gy', 'gx')
Outputs:
- rotated: float32 [2, 2, 2048, 1024], P(None, 'gy', 'gx', 'gz')
- exit_wave: float32 [2, 2, 2048], P(None, 'gy', 'gx')
Inputs may be any that keep to these rules, and one draw needn't show every extreme that they name: `depth_hops`: in every row of every angle, both -256 and 256 occur. `column_hops`: in every angle, both -128 and 128 occur. `angle_index`: each angle occurs once.
All inputs are finite; a program needn't handle non-finite values.
Results may differ from a plain program's by a relative error of at most 0.000028.
Values sent between devices are 32-bit elements; how exact they have to be, the bound alone decides.
No kernel may reach another device: no remote copies, remote signals or barrier semaphores. Data moves between devices by JAX's collectives and lax.ppermute only.
A program may use at most 64 MiB of HBM per device.

v0:
```python
import math

import jax
import jax.numpy as jnp
from jax import lax
from jax.sharding import PartitionSpec as P

HOPS_X = 2
HOPS_Z = 1
SLICES = 64


def shifted(block, axis, distance):
    devices = range(lax.axis_size(axis))
    route = [((i - distance) % len(devices), i) for i in devices]
    return lax.ppermute(block, axis, route)


def joined(value, axis, combine):
    everything = jax.tree.map(lambda part: lax.all_gather(part, axis), value)
    first = jax.tree.map(lambda part: part[0], everything)

    def step(k, so_far):
        return combine(so_far, jax.tree.map(lambda part: part[k], everything))

    return lax.fori_loop(1, lax.axis_size(axis), step, first)


def apply_taps(extended, source_rows, tap_weights, length):
    shaped = jnp.broadcast_to(
        source_rows[None, None], (extended.shape[0], extended.shape[1]) + source_rows.shape
    )
    window = jnp.take_along_axis(extended, shaped, axis=2)
    summed = None
    for tap_number in range(8):
        term = (
            tap_weights[tap_number][None, None, None, :]
            * window[:, :, tap_number : tap_number + length]
        )
        summed = term if summed is None else summed + term
    return summed


def near_block(slab_field, stride, along_x):
    if along_x:
        return shifted(slab_field, "gx", stride)
    return shifted(slab_field, "gz", stride)


def shear_pass(slab_field, hop_counts, tap_weights, along_x):
    length = slab_field.shape[2]
    places = jnp.arange(length + 7, dtype=jnp.int32)[:, None]
    hop_counts = hop_counts[None, :]
    largest = HOPS_X if along_x else HOPS_Z
    pieces = []
    for offset in range(-largest - 1, largest + 2):
        pieces.append(slab_field if offset == 0 else near_block(slab_field, -offset, along_x))
    extended = jnp.concatenate(pieces, axis=2)
    source_rows = (largest + 1) * length + places - hop_counts - 3
    return apply_taps(extended, source_rows, tap_weights, length)


def complex_product(earlier, later):
    return (
        earlier[0] * later[0] - earlier[1] * later[1],
        earlier[0] * later[1] + earlier[1] * later[0],
    )


def local(object_slab, depth_hops, depth_taps, column_hops, column_taps, angle_index, illumination):
    which = angle_index[0]
    chosen_hops = depth_hops[which]
    chosen_taps = depth_taps[which]
    first = shear_pass(object_slab, chosen_hops[0], chosen_taps[0], True)
    second = jnp.swapaxes(
        shear_pass(jnp.swapaxes(first, 2, 3), column_hops[which], column_taps[which], False), 2, 3
    )
    rotated = shear_pass(second, chosen_hops[1], chosen_taps[1], True)
    row_count = rotated.shape[1]
    column_count = rotated.shape[2]
    depth_cells = rotated.shape[3] * lax.axis_size("gz")
    slice_depth = depth_cells // SLICES
    local_slices = rotated.shape[3] // slice_depth
    projected = rotated.reshape(2, row_count, column_count, local_slices, slice_depth).sum(axis=-1)
    strength = 0.5 / math.sqrt(depth_cells)
    magnitude = jnp.exp(-strength * projected[1])
    slice_real = magnitude * jnp.cos(strength * projected[0])
    slice_imag = magnitude * jnp.sin(strength * projected[0])
    trans_real = jnp.ones((row_count, column_count), jnp.float32)
    trans_imag = jnp.zeros((row_count, column_count), jnp.float32)
    for slice_number in range(local_slices):
        trans_real, trans_imag = complex_product(
            (trans_real, trans_imag),
            (slice_real[:, :, slice_number], slice_imag[:, :, slice_number]),
        )
    trans_real, trans_imag = joined((trans_real, trans_imag), "gz", complex_product)
    wave_real = illumination[0] * trans_real - illumination[1] * trans_imag
    wave_imag = illumination[0] * trans_imag + illumination[1] * trans_real
    local_power = jnp.sum(wave_real * wave_real + wave_imag * wave_imag)
    cell_count = row_count * lax.axis_size("gy") * column_count * lax.axis_size("gx")
    total_power = lax.psum(local_power, ("gx", "gy")) / cell_count
    factor = 1.0 / jnp.sqrt(total_power + 1e-06)
    exit_wave = jnp.stack([wave_real * factor, wave_imag * factor])
    return (rotated, exit_wave)


def solution(mesh):
    return jax.shard_map(
        local,
        mesh=mesh,
        in_specs=(
            P(None, "gy", "gx", "gz"),
            P(None, None, "gz"),
            P(None, None, None, "gz"),
            P(None, "gx"),
            P(None, None, "gx"),
            P(),
            P(None, "gy", "gx"),
        ),
        out_specs=(P(None, "gy", "gx", "gz"), P(None, "gy", "gx")),
        check_vma=False,
    )
```

profile of v0, /device:TPU:1, one launch (start us, length us, event | category | flops | bytes accessed | tf_op | source)
XLA Modules:
  0.0 1063.1 jit_solution(9234937908941943979)
XLA Ops:
  0.7 4.2 collective-permute-start
  5.7 4.8 collective-permute-start.4
  14.3 1.1 fusion.41
  15.4 1.2 collective-permute-start.5
  16.7 4.7 collective-permute-done.5
  21.4 260.5 %gather_fusion.1 = f32[34560]{0:T(1024)S(1)} fusion(f32[2,896,128]{2,1,0:T(8,128)S(1)} %bitcast.267, s32[34560]{0:T(1024)S(1)} %reshape.961), kind=kCustom, calls=%fused_computation.clone | custom fusion | bytes 691200 | tf_op jit(solution)/shard_map/jit(take_along_axis)/gather | solution.py:33
  282.0 3.1 collective-permute-start.6
  285.1 1.6 collective-permute-start.7
  286.7 1.1 collective-permute-start.8
  287.9 2.3 collective-permute-start.9
  290.2 2.4 collective-permute-done.6
  292.6 4.6 collective-permute-done.7
  297.4 2.2 collective-permute-done.9
  299.5 326.5 %gather_fusion = f32[34560]{0:T(1024)S(1)} fusion(f32[2,640,128]{1,2,0:T(8,128)S(1)} %bitcast.266, s32[34560]{0:T(1024)S(1)} %reshape.940), kind=kCustom, calls=%fused_computation.2 | custom fusion | bytes 691200 | tf_op jit(solution)/shard_map/jit(take_along_axis)/gather | solution.py:33
  626.2 0.8 collective-permute-start.10
  627.0 4.3 collective-permute-start.11
  631.3 1.2 collective-permute-start.12
  632.5 1.1 collective-permute-start.14
  633.7 3.9 collective-permute-done.10
  638.1 5.4 collective-permute-done.15
  643.5 326.5 %gather_fusion.2 = f32[34560]{0:T(1024)S(1)} fusion(f32[2,896,128]{1,2,0:T(8,128)S(1)} %bitcast.268, s32[34560]{0:T(1024)S(1)} %reshape.967), kind=kCustom, calls=%fused_computation.1.clone | custom fusion | bytes 691200 | tf_op jit(solution)/shard_map/jit(take_along_axis)/gather | solution.py:33
  971.2 9.7 all_gather.8
  980.9 11.1 %all_gather.9 = f32[8,1,128]{2,1,0:T(1,128)S(1)} all-gather(f32[1,1,128]{2,1,0:T(1,128)S(1)} %get-tuple-element.157), channel_id=1, replica_groups=mesh['gx'=16,'gz'=8,'gy'=2] {'gz'}, dimensions={0}, use_global_device_ids=true | all-gather | bytes 4608 | tf_op jit(solution)/shard_map/all_gather | solution.py:20
  992.9 68.9 %psum.7 = f32[]{:T(128)} all-reduce(f32[]{:T(128)} %get-tuple-element.154), channel_id=1, replica_groups=mesh['gx'=16,'gz'=8,'gy'=2] {'gx','gy'}, use_global_device_ids=true, to_apply=%region_4.6 | all-reduce | flops 1 | bytes 8 | tf_op jit(solution)/shard_map/psum | solution.py:101
  (88 shorter events, 6.5 us)
Async XLA Ops:
  0.6 14.7 %copy-start = (f32[16,8,128]{2,1,0:T(8,128)S(1)}, f32[16,8,128]{2,1,0:T(8,128)}, u32[]{:S(2)}) copy-start(f32[16,8,128]{2,1,0:T(8,128)} %param.15) | copy-start | bytes 196612
  0.6 14.7 %copy-start.1 = (f32[2,1,128,128]{3,2,1,0:T(8,128)S(1)}, f32[2,1,128,128]{3,2,1,0:T(8,128)}, u32[]{:S(2)}) copy-start(f32[2,1,128,128]{3,2,1,0:T(8,128)} %param.11) | copy-start | bytes 393220
  0.7 14.7 %collective-permute-start = (f32[2,1,128,128]{3,2,0,1:T(8,128)}, f32[2,1,128,128]{3,2,0,1:T(8,128)S(1)}, u32[]{:S(2)}, u32[]{:S(2)}) collective-permute-start(f32[2,1,128,128]{3,2,0,1:T(8,128)} %bitcast.270), channel_id=1, source_target_pairs={{208,0},{224,16},{240,32},{0,48},{16,64},{32,80},{48,96},{64,112},... | collective-permute-start | bytes 393224 | tf_op jit(solution)/shard_map/ppermute | solution.py:16
  4.9 11.7 %collective-permute-start.1 = (f32[2,1,128,128]{3,2,0,1:T(8,128)}, f32[2,1,128,128]{3,2,0,1:T(8,128)S(1)}, u32[]{:S(2)}, u32[]{:S(2)}) collective-permute-start(f32[2,1,128,128]{3,2,0,1:T(8,128)} %bitcast.271), channel_id=1, source_target_pairs={{224,0},{240,16},{0,32},{16,48},{32,64},{48,80},{64,96},{80,112},{... | collective-permute-start | bytes 393224 | tf_op jit(solution)/shard_map/ppermute | solution.py:16
  5.2 11.4 %collective-permute-start.2 = (f32[2,1,128,128]{3,2,0,1:T(8,128)}, f32[2,1,128,128]{3,2,0,1:T(8,128)S(1)}, u32[]{:S(2)}, u32[]{:S(2)}) collective-permute-start(f32[2,1,128,128]{3,2,0,1:T(8,128)} %bitcast.272), channel_id=1, source_target_pairs={{240,0},{0,16},{16,32},{32,48},{48,64},{64,80},{80,96},{96,112},{1... | collective-permute-start | bytes 393224 | tf_op jit(solution)/shard_map/ppermute | solution.py:16
  5.5 11.2 %collective-permute-start.3 = (f32[2,1,128,128]{3,2,0,1:T(8,128)}, f32[2,1,128,128]{3,2,0,1:T(8,128)S(1)}, u32[]{:S(2)}, u32[]{:S(2)}) collective-permute-start(f32[2,1,128,128]{3,2,0,1:T(8,128)} %bitcast.273), channel_id=1, source_target_pairs={{16,0},{32,16},{48,32},{64,48},{80,64},{96,80},{112,96},{128,112},... | collective-permute-start | bytes 393224 | tf_op jit(solution)/shard_map/ppermute | solution.py:16
  5.7 11.0 %collective-permute-start.4 = (f32[2,1,128,128]{3,2,0,1:T(8,128)}, f32[2,1,128,128]{3,2,0,1:T(8,128)S(1)}, u32[]{:S(2)}, u32[]{:S(2)}) collective-permute-start(f32[2,1,128,128]{3,2,0,1:T(8,128)} %bitcast.274), channel_id=1, source_target_pairs={{32,0},{48,16},{64,32},{80,48},{96,64},{112,80},{128,96},{144,112}... | collective-permute-start | bytes 393224 | tf_op jit(solution)/shard_map/ppermute | solution.py:16
  15.4 6.0 collective-permute-start.5
  282.0 10.6 collective-permute-start.6
  285.1 12.1 %collective-permute-start.7 = (f32[2,1,128,128]{2,3,0,1:T(8,128)S(1)}, f32[2,1,128,128]{2,3,0,1:T(8,128)S(1)}, u32[]{:S(2)}, u32[]{:S(2)}) collective-permute-start(f32[2,1,128,128]{2,3,0,1:T(8,128)S(1)} %fusion.31), channel_id=1, source_target_pairs={{14,0},{0,2},{2,4},{4,6},{6,8},{8,10},{10,12},{12,14},{15,1},{1,3}... | collective-permute-start | bytes 393224 | tf_op jit(solution)/shard_map/ppermute | solution.py:16
  286.7 10.6 collective-permute-start.8
  287.9 11.6 %collective-permute-start.9 = (f32[2,1,128,128]{2,3,0,1:T(8,128)S(1)}, f32[2,1,128,128]{2,3,0,1:T(8,128)S(1)}, u32[]{:S(2)}, u32[]{:S(2)}) collective-permute-start(f32[2,1,128,128]{2,3,0,1:T(8,128)S(1)} %fusion.31), channel_id=1, source_target_pairs={{4,0},{6,2},{8,4},{10,6},{12,8},{14,10},{0,12},{2,14},{5,1},{7,3},... | collective-permute-start | bytes 393224 | tf_op jit(solution)/shard_map/ppermute | solution.py:16
  626.2 11.4 %collective-permute-start.10 = (f32[2,1,128,128]{2,3,0,1:T(8,128)S(1)}, f32[2,1,128,128]{2,3,0,1:T(8,128)S(1)}, u32[]{:S(2)}, u32[]{:S(2)}) collective-permute-start(f32[2,1,128,128]{2,3,0,1:T(8,128)S(1)} %fusion.23), channel_id=1, source_target_pairs={{208,0},{224,16},{240,32},{0,48},{16,64},{32,80},{48,96},{64,112},... | collective-permute-start | bytes 393224 | tf_op jit(solution)/shard_map/ppermute | solution.py:16
  627.0 10.8 %collective-permute-start.11 = (f32[2,1,128,128]{2,3,0,1:T(8,128)S(1)}, f32[2,1,128,128]{2,3,0,1:T(8,128)S(1)}, u32[]{:S(2)}, u32[]{:S(2)}) collective-permute-start(f32[2,1,128,128]{2,3,0,1:T(8,128)S(1)} %fusion.23), channel_id=1, source_target_pairs={{224,0},{240,16},{0,32},{16,48},{32,64},{48,80},{64,96},{80,112},{... | collective-permute-start | bytes 393224 | tf_op jit(solution)/shard_map/ppermute | solution.py:16
  631.3 6.5 collective-permute-start.12
  632.5 5.6 collective-permute-start.13
  632.5 5.6 collective-permute-start.14
  637.6 5.9 collective-permute-start.15
  970.8 21.5 %copy-start.2 = (f32[2,1,128]{2,1,0:T(1,128)S(1)}, f32[2,1,128]{2,1,0:T(1,128)}, u32[]{:S(2)}) copy-start(f32[2,1,128]{2,1,0:T(1,128)} %param.17) | copy-start | bytes 3076
where the time goes:
time: 1060 us
  local copies, waits for them, and re-layouts  916 us (86%)
  blocking collectives  89.8 us (8%)
  starting transfers between devices  26.6 us (3%)
  waiting for transfers between devices  23.3 us (2%)
    gather x9, local copies, waits for them, and re-layouts, apply_taps(): window = jnp.take_along_axis(extended, shaped, axis=2)  913 us
    psum x1, blocking collectives, local(): total_power = lax.psum(local_power, ('gx', 'gy')) / cell_count  68.9 us
    ppermute x16, starting transfers between devices, shifted(): return lax.ppermute(block, axis, route)  26.6 us
    ppermute x16, waiting for transfers between devices, shifted(): return lax.ppermute(block, axis, route)  23.3 us
  transfers between devices with their start and end apart: 16, of which 7 were waited for; matrix products, arithmetic and copies ran while one was open for 0% of the time, Pallas kernels for 0%

commit v1 on v0

v1 whole, which is shorter than its diff:
```python
import functools
import math

import jax
import jax.numpy as jnp
from jax import lax
from jax.experimental import pallas as pl
from jax.experimental.pallas import tpu as pltpu
from jax.sharding import PartitionSpec as P

B = 128
SPAN_X = 256
SPAN_Z = 128
VMEM = pltpu.CompilerParams(vmem_limit_bytes=32 * 1024 * 1024)


def permuted(value, axis, target):
    return lax.ppermute(value, axis, [(i, target(i)) for i in range(lax.axis_size(axis))])


def pairings(count):
    return (
        lambda c: c ^ 1,
        lambda c: (c + 1 if c & 1 else c - 1) % count,
        lambda c: c ^ 2,
        lambda c: (c + 2 if c & 2 else c - 2) % count,
    )


def barrel(ref, kept, top, shifts):
    for bit in range(top, -1, -1):
        step = 1 << bit
        rows = kept if bit == top else -(-(kept + step - 1) // 8) * 8
        moved = (shifts & step) != 0
        for start in range(0, rows, 64):
            size = min(64, rows - start)
            here = ref[pl.ds(start, size), :]
            there = ref[pl.ds(start + step, size), :]
            ref[pl.ds(start, size), :] = jnp.where(moved, there, here)


def tap_sum(ref, first_row, size, taps):
    total = None
    for k in range(8):
        term = taps[k : k + 1, :] * ref[pl.ds(first_row + k, size), :]
        total = term if total is None else total + term
    return total


def assemble(ext, at, size, flag, when_set, when_clear, row_set, row_clear):
    @pl.when(flag == 1)
    def _():
        ext[pl.ds(at, size), :] = when_set[pl.ds(row_set, size), :]

    @pl.when(flag == 0)
    def _():
        ext[pl.ds(at, size), :] = when_clear[pl.ds(row_clear, size), :]


def first_kernel(flags, own, near_a, near_b, far_a, far_b, hops, taps, out, edges, columns, ext, rows):
    odd, second_bit = flags[0], flags[1]
    ext[0:8, :] = jnp.zeros((8, B), jnp.float32)
    ext[792:800, :] = jnp.zeros((8, B), jnp.float32)
    assemble(ext, 8, 8, second_bit, far_a, far_b, 8, 8)
    assemble(ext, 16, 256, odd, near_a, near_b, 0, 0)
    ext[272:528, :] = own[0:256, :]
    assemble(ext, 528, 256, odd, near_b, near_a, 0, 0)
    assemble(ext, 784, 8, second_bit, far_b, far_a, 0, 0)
    barrel(ext, 288, 9, SPAN_X - hops[...])
    weights = taps[...]
    for start in range(0, 256, 64):
        rows[pl.ds(start, 64), :] = tap_sum(ext, start + 13, 64, weights)
    rows[256:264, :] = tap_sum(ext, 269, 8, weights)
    rows[264:272, :] = tap_sum(ext, 5, 8, weights)
    rows[272:384, :] = jnp.zeros((112, B), jnp.float32)
    for tile in range(3):
        turned = rows[pl.ds(tile * B, B), :].T
        out[tile] = turned
        edges[tile, 0:8, :] = turned[0:8, :]
        edges[tile, 8:16, :] = turned[120:128, :]
    columns[0] = own[256:272, :]
    columns[1] = own[272:288, :]
    lane = lax.broadcasted_iota(jnp.int32, (16, B), 1)

    @pl.when(odd == 1)
    def _():
        low = pltpu.roll(near_a[272:288, :], 16, 1)
        columns[2] = jnp.where(lane < 8, near_b[256:272, :], low)

    @pl.when(odd == 0)
    def _():
        low = pltpu.roll(near_b[272:288, :], 16, 1)
        columns[2] = jnp.where(lane < 8, near_a[256:272, :], low)


def second_kernel(flags, own, near_a, near_b, far_a, far_b, columns, out, ext):
    odd, second_bit = flags[2], flags[3]
    for tile in range(3):
        e = ext.at[tile]
        t = tile
        assemble(e, 0, 8, second_bit, far_a.at[t], far_b.at[t], 8, 8)
        assemble(e, 8, 128, odd, near_a.at[t], near_b.at[t], 0, 0)
        e[136:264, :] = own[t]
        assemble(e, 264, 128, odd, near_b.at[t], near_a.at[t], 0, 0)
        assemble(e, 392, 8, second_bit, far_b.at[t], far_a.at[t], 0, 0)
        weights = columns[t]
        barrel(e, 144, 8, SPAN_Z - weights[8:9, :].astype(jnp.int32))
        summed = tap_sum(e, 5, 128, weights).T
        if tile < 2:
            out[pl.ds(tile * B, B), :] = summed
        else:
            out[256:272, :] = summed[0:16, :]


def third_kernel(flags, own, near_a, near_b, hops, taps, keep, send, ext):
    odd, core = flags[0], flags[4]
    ext[0:8, :] = jnp.zeros((8, B), jnp.float32)
    ext[792:800, :] = jnp.zeros((8, B), jnp.float32)
    assemble(ext, 8, 8, odd, near_a, near_b, 264, 264)
    assemble(ext, 16, 256, odd, near_a, near_b, 0, 0)
    ext[272:528, :] = own[0:256, :]
    assemble(ext, 528, 264, odd, near_b, near_a, 0, 0)
    barrel(ext, 288, 9, SPAN_X - hops[...])
    weights = taps[...]
    low = tap_sum(ext, 13, 128, weights)
    high = tap_sum(ext, 13 + 128, 128, weights)
    keep[...] = jnp.where(core == 0, low, high)
    send[...] = jnp.where(core == 0, high, low)


def column_sum_kernel(own, hops, taps, out, ext, moved_ref):
    weights = taps[...]
    ext[0:8, :] = jnp.zeros((8, B), jnp.float32)
    ext[8:264, :] = own[0:256, :]
    ext[264:280, :] = jnp.zeros((16, B), jnp.float32)
    moved_ref[...] = jnp.zeros((640, B), jnp.float32)
    for start in range(0, 264, 88):
        moved_ref[pl.ds(B + start, 88), :] = tap_sum(ext, start + 1, 88, weights)
    shifts = SPAN_X + hops[...]
    for bit in range(7):
        step = 1 << bit
        moved = (shifts & step) != 0
        rows = -(-(264 + 2 * step - 1) // 8) * 8
        for start in reversed(range(0, rows, 64)):
            size = min(64, rows - start)
            here = moved_ref[pl.ds(B + start, size), :]
            there = moved_ref[pl.ds(B + start - step, size), :]
            moved_ref[pl.ds(B + start, size), :] = jnp.where(moved, there, here)
    chosen = lax.broadcasted_iota(jnp.int32, (8, B), 0) == (shifts >> 7)
    sums = lax.dot_general(
        chosen.astype(jnp.float32),
        moved_ref[B:, :],
        (((1,), (1,)), ((), ())),
        precision=lax.Precision.HIGHEST,
        preferred_element_type=jnp.float32,
    )
    out[...] = jnp.zeros((8, B), jnp.float32)
    for block in range(5):
        for tile in range(4):
            if block + tile < 7:
                row = block + tile
                out[row : row + 1, :] += sums[block : block + 1, tile * B : (tile + 1) * B]


def exit_kernel(strength, cells, flags, gathered, illumination, out, acc, loud, proj):
    x_place, y_place = flags[5], flags[6]
    columns = gathered.shape[0] // 2
    row = lax.broadcasted_iota(jnp.int32, (8, B), 0)
    lane = lax.broadcasted_iota(jnp.int32, (columns, B), 1)
    power = None
    for y in range(2):
        for m in range(columns):
            loud[m : m + 1, :] = gathered[2 * m + y, 7:8, :]
        for channel in range(2):
            acc[...] = jnp.zeros(acc.shape, jnp.float32)
            for c in range(columns // 2):
                piece = jnp.where(row < 7, gathered[(2 * c + channel) * 2 + y], 0.0)
                acc[pl.ds(2 * c, 8), :] += piece
            acc[0:8, :] += acc[columns : columns + 8, :]
            acc[columns : columns + 8, :] = acc[0:8, :]
            below = pltpu.roll(acc[2 : columns + 2, :], B - 4, 1)
            above = pltpu.roll(acc[3 : columns + 3, :], B - 4, 1)
            proj[channel, y] = jnp.where(lane < B - 4, below, above)
        root = jnp.exp((-0.5 * strength) * proj[1, y])
        size = 2.0 * ((loud[...] * root) * root)
        part = size * size
        power = part if power is None else power + part
    power = jnp.sum(power, keepdims=True) / cells
    factor = 2.0 / jnp.sqrt(power + 1e-06)
    angle = strength * proj[0, y_place, pl.ds(x_place, 1), :]
    root = jnp.exp((-0.5 * strength) * proj[1, y_place, pl.ds(x_place, 1), :])
    turn_real, turn_imag = jnp.cos(angle), jnp.sin(angle)
    real, imag = 0.5 * illumination[0:1, :], 0.5 * illumination[1:2, :]
    out[0:1, :] = (((real * turn_real - imag * turn_imag) * root) * root) * factor
    out[1:2, :] = (((real * turn_imag + imag * turn_real) * root) * root) * factor


SMEM_SPEC = pl.BlockSpec(memory_space=pltpu.SMEM)
VMEM_SPEC = pl.BlockSpec(memory_space=pltpu.VMEM)


def call(kernel, name, scalars, arrays, outs, scratch):
    f32 = lambda shape: jax.ShapeDtypeStruct(shape, jnp.float32)
    result = pl.pallas_call(
        kernel,
        out_shape=[f32(shape) for shape in outs],
        in_specs=[SMEM_SPEC] * len(scalars) + [VMEM_SPEC] * len(arrays),
        out_specs=[VMEM_SPEC] * len(outs),
        scratch_shapes=[pltpu.VMEM(shape, jnp.float32) for shape in scratch],
        compiler_params=VMEM,
        name=name,
    )(*scalars, *arrays)
    return result[0] if len(outs) == 1 else result


def half_size(illumination):
    real, imag = jnp.abs(illumination[0]), jnp.abs(illumination[1])
    large, small = jnp.maximum(real, imag), jnp.minimum(real, imag)
    ratio = small / jnp.where(large > 0, large, 1.0)
    return (0.5 * large) * jnp.sqrt(1.0 + ratio * ratio)


def everywhere(value, axes, count):
    copies = jnp.broadcast_to(value[None], (count,) + value.shape)
    return lax.all_to_all(copies, axes, 0, 0, tiled=True)


def local(object_slab, depth_hops, depth_taps, column_hops, column_taps, angle_index, illumination):
    which = angle_index[0]
    gx, gz, gy = lax.axis_index("gx"), lax.axis_index("gz"), lax.axis_index("gy")
    size_x, size_z, size_y = lax.axis_size("gx"), lax.axis_size("gz"), lax.axis_size("gy")
    chip, core = gx // 2, gx % 2
    flags = jnp.stack(
        [chip & 1, (chip >> 1) & 1, gz & 1, (gz >> 1) & 1, core, gx, gy, gy]
    ).astype(jnp.int32)
    hops, taps = depth_hops[which], depth_taps[which]
    columns = jnp.concatenate(
        [
            column_taps[which],
            column_hops[which].astype(jnp.float32)[None],
            jnp.zeros((7, B), jnp.float32),
        ]
    )
    slab = object_slab[:, 0]
    mine = jnp.concatenate([jnp.where(core == 0, slab[0], slab[1]), columns])
    theirs = jnp.concatenate([jnp.where(core == 0, slab[1], slab[0]), columns])
    swap = lambda i: i ^ 1
    got = permuted(theirs, "gx", swap)
    low, high = jnp.where(core == 0, mine, got), jnp.where(core == 0, got, mine)
    own = jnp.concatenate([low[:B], high[:B], low[B:], high[B:]])
    ring_x = [
        lambda i, f=f: 2 * f(i // 2) + i % 2 for f in pairings(size_x // 2)
    ]
    ring_z = pairings(size_z)
    edges = jnp.concatenate([own[0:8], own[248:256]])
    received = [permuted(own, "gx", ring_x[0]), permuted(own, "gx", ring_x[1])]
    received += [permuted(edges, "gx", ring_x[2]), permuted(edges, "gx", ring_x[3])]
    first, first_edges, columns = call(
        first_kernel,
        "first_shear",
        [flags],
        [own, *received, hops[0:1], taps[0]],
        [(3, B, B), (3, 16, B), (3, 16, B)],
        [(800, B), (384, B)],
    )
    received = [permuted(first, "gz", ring_z[0]), permuted(first, "gz", ring_z[1])]
    received += [permuted(first_edges, "gz", ring_z[2]), permuted(first_edges, "gz", ring_z[3])]
    second = call(
        second_kernel,
        "second_shear",
        [flags],
        [first, *received, columns],
        [(272, B)],
        [(3, 400, B)],
    )
    received = [permuted(second, "gx", ring_x[0]), permuted(second, "gx", ring_x[1])]
    sums = call(
        column_sum_kernel,
        "depth_sum",
        [],
        [second, hops[1:2], taps[1]],
        [(8, B)],
        [(280, B), (640, B)],
    )
    sums = everywhere(sums, "gz", size_z).sum(axis=0)
    sums = jnp.concatenate([sums[:7], half_size(illumination[:, 0])[None]])
    gathered = everywhere(sums, ("gx", "gy"), size_x * size_y)
    keep, send = call(
        third_kernel,
        "third_shear",
        [flags],
        [second, *received, hops[1:2], taps[1]],
        [(B, B), (B, B)],
        [(800, B)],
    )
    got = permuted(send, "gx", swap)
    rotated = jnp.where(core == 0, jnp.stack([keep, got]), jnp.stack([got, keep]))
    exit_wave = call(
        functools.partial(
            exit_kernel, 0.5 / math.sqrt(B * size_z), float(size_x * B * size_y)
        ),
        "exit_wave",
        [flags],
        [gathered, illumination[:, 0]],
        [(2, B)],
        [(size_x + 8, B), (size_x, B), (2, 2, size_x, B)],
    )
    return (rotated[:, None], exit_wave[:, None])


def solution(mesh):
    return jax.shard_map(
        local,
        mesh=mesh,
        in_specs=(
            P(None, "gy", "gx", "gz"),
            P(None, None, "gz"),
            P(None, None, None, "gz"),
            P(None, "gx"),
            P(None, None, "gx"),
            P(),
            P(None, "gy", "gx"),
        ),
        out_specs=(P(None, "gy", "gx", "gz"), P(None, "gy", "gx")),
        check_vma=False,
    )
```

time: 1060 us -> 65.7 us (0.06)
  local copies, waits for them, and re-layouts: 916 us -> 3.57 us
  blocking collectives: 89.8 us -> 0 us
    gather x9 -> x0, local copies, waits for them, and re-layouts: 913 us -> none  [apply_taps(): window = jnp.take_along_axis(extended, shaped, axis=2)]
    psum x1 -> x0, blocking collectives: 68.9 us -> none  [local(): total_power = lax.psum(local_power, ('gx', 'gy')) / cell_count]
    all_gather x2 -> x0, blocking collectives: 20.9 us -> none  [joined(): everything = jax.tree.map(lambda part: lax.all_gather(part, axis), value)]
    ppermute x16 -> x12, waiting for transfers between devices: 23.3 us -> 6.5 us  [permuted(): lax.ppermute(value, axis, [(i, target(i)) for i in range(lax.axis_size(ax...]
    all_to_all x0 -> x2, starting transfers between devices: none -> 15.4 us  [everywhere(): return lax.all_to_all(copies, axes, 0, 0, tiled=True)]
    all_to_all x0 -> x2, waiting for transfers between devices: none -> 10.6 us  [everywhere(): return lax.all_to_all(copies, axes, 0, 0, tiled=True)]
    ppermute x16 -> x12, starting transfers between devices: 26.6 us -> 21 us  [permuted(): lax.ppermute(value, axis, [(i, target(i)) for i in range(lax.axis_size(ax...]
  transfers between devices with their start and end apart: 16 -> 14, of which waited for: 7 -> 7; matrix products, arithmetic and copies ran while one was open for 0% -> 3% of each run, Pallas kernels for 0% -> 4%
where the time goes in v1:
time: 65.7 us; the launch traced here: 65.3 us
  starting transfers between devices  36.4 us (55%)
  waiting for transfers between devices  17.1 us (26%)
  Pallas kernels  4.82 us (7%)
  local copies, waits for them, and re-layouts  3.57 us (5%)
  other arithmetic  2.46 us (4%)
  between operations  0.94 us (1%)
    ppermute x12, starting transfers between devices, permuted(): lax.ppermute(value, axis, [(i, target(i)) for i in range(lax.axis_size(ax...  21 us
    all_to_all x2, starting transfers between devices, everywhere(): return lax.all_to_all(copies, axes, 0, 0, tiled=True)  15.4 us
    all_to_all x2, waiting for transfers between devices, everywhere(): return lax.all_to_all(copies, axes, 0, 0, tiled=True)  10.6 us
    ppermute x12, waiting for transfers between devices, permuted(): lax.ppermute(value, axis, [(i, target(i)) for i in range(lax.axis_size(ax...  6.5 us
    pallas_call x5, Pallas kernels, call(): pl.pallas_call(kernel, out_shape=[f32(shape) for shape in outs], in_specs...  4.82 us
  transfers between devices with their start and end apart: 14, of which 7 were waited for; matrix products, arithmetic and copies ran while one was open for 3% of the time, Pallas kernels for 4%

profile of v1, /device:TPU:1, one launch (start us, length us, event | category | flops | bytes accessed | tf_op | source)
XLA Modules:
  0.0 65.3 jit_solution(3985112070458335543)
XLA Ops:
  0.7 0.7 %copy-done.2 = s32[16]{0:T(128)S(1)} copy-done((s32[16]{0:T(128)S(1)}, s32[16]{0:T(128)}, u32[]{:S(2)}) %copy-start.2) | copy-done | bytes 88
  1.5 0.7 %fusion.4 = f32[1,128]{1,0:T(1,128)S(1)} fusion(s32[16,128]{1,0:T(8,128)} %param.10, s32[]{:T(128)S(6)} %select_n.80), kind=kLoop, calls=%fused_computation.20 | loop fusion | flops 128 | bytes 1028 | tf_op jit(solution)/shard_map/convert_element_type | solution.py:240
  2.2 0.9 %select_bitcast_fusion.1 = (f32[128,128]{1,0:T(8,128)S(1)}, f32[128,128]{1,0:T(8,128)S(1)}) fusion(f32[2,1,128,128]{3,2,1,0:T(8,128)} %param.7, pred[]{:T(512)S(6)} %eq.4), kind=kLoop, calls=%fused_computation.9 | loop fusion | flops 32768 | bytes 262145 | tf_op jit(solution)/shard_map/jit(_where)/select_n | solution.py:245
  3.2 3.3 %collective-permute-start = (f32[144,128]{1,0:T(8,128)S(1)}, f32[144,128]{1,0:T(8,128)S(1)}, u32[]{:S(2)}, u32[]{:S(2)}) collective-permute-start(f32[144,128]{1,0:T(8,128)S(1)} %fusion.1), channel_id=1, source_target_pairs={{0,16},{16,0},{32,48},{48,32},{64,80},{80,64},{96,112},{112,96},{1... | collective-permute-start | bytes 221192 | tf_op jit(solution)/shard_map/ppermute | solution.py:18
  6.6 0.7 %constant_dynamic-slice_fusion = s32[1,2,128]{2,1,0:T(2,128)S(1)} fusion(s32[16,2,128]{2,1,0:T(2,128)} %param.8, s32[]{:T(128)S(6)} %select_n.80), kind=kLoop, calls=%fused_computation.18 | loop fusion | bytes 2052 | tf_op jit(solution)/shard_map/dynamic_slice | solution.py:236
  7.8 3.9 %collective-permute-start.2 = (f32[288,128]{1,0:T(8,128)S(1)}, f32[288,128]{1,0:T(8,128)S(1)}, u32[]{:S(2)}, u32[]{:S(2)}) collective-permute-start(f32[288,128]{1,0:T(8,128)S(1)} %pad_maximum_fusion.own), channel_id=1, source_target_pairs={{0,224},{16,240},{32,64},{48,80},{64,32},{80,48},{96,128},{112,144... | collective-permute-start | bytes 442376 | tf_op jit(solution)/shard_map/ppermute | solution.py:18
  11.7 2.7 %collective-permute-start.4 = (f32[16,128]{1,0:T(8,128)S(1)}, f32[16,128]{1,0:T(8,128)S(1)}, u32[]{:S(2)}, u32[]{:S(2)}) collective-permute-start(f32[16,128]{1,0:T(8,128)S(1)} %pad_maximum_fusion.5), channel_id=1, source_target_pairs={{0,192},{16,208},{32,224},{48,240},{64,128},{80,144},{96,160},{112... | collective-permute-start | bytes 24584 | tf_op jit(solution)/shard_map/ppermute | solution.py:18
  14.4 0.7 %dynamic-slice_bitcast_fusion = (f32[8,128]{1,0:T(8,128)S(1)}, f32[8,128]{1,0:T(8,128)S(1)}) fusion(f32[16,2,8,128]{3,2,1,0:T(8,128)} %param.9, s32[]{:T(128)S(6)} %select_n.80, s32[]{:T(128)S(6)} %add.25), kind=kLoop, calls=%fused_computation.13 | loop fusion | bytes 16392 | tf_op jit(solution)/shard_map/squeeze | solution.py:292
  15.2 0.8 %collective-permute-done.3.far_a = f32[16,128]{1,0:T(8,128)S(1)} collective-permute-done((f32[16,128]{1,0:T(8,128)S(1)}, f32[16,128]{1,0:T(8,128)S(1)}, u32[]{:S(2)}, u32[]{:S(2)}) %collective-permute-start.3) | collective-permute-done | bytes 8224 | tf_op jit(solution)/shard_map/ppermute | solution.py:18
  16.0 2.1 %collective-permute-done.4.far_b = f32[16,128]{1,0:T(8,128)S(1)} collective-permute-done((f32[16,128]{1,0:T(8,128)S(1)}, f32[16,128]{1,0:T(8,128)S(1)}, u32[]{:S(2)}, u32[]{:S(2)}) %collective-permute-start.4) | collective-permute-done | bytes 8224 | tf_op jit(solution)/shard_map/ppermute | solution.py:18
  18.1 0.9 %first_shear.1 = (f32[3,128,128]{2,1,0:T(8,128)S(1)}, f32[3,16,128]{2,1,0:T(8,128)S(1)}, f32[3,16,128]{2,1,0:T(8,128)S(1)}) custom-call(s32[8]{0:T(128)S(1)} %stack.46.flags, f32[288,128]{1,0:T(8,128)S(1)} %pad_maximum_fusion.own, f32[288,128]{1,0:T(8,128)S(1)} %collective-permute-done.1.near_a, f32[288,128]{1,0:T(8,128)S(1)} %collective-permute-done.2.near_b, ...), custom_call_target="tpu_custom_call" | custom-call | tf_op jit(solution)/shard_map/first_shear/pallas_call | solution.py:204
  19.0 1.7 %collective-permute-start.5 = (f32[3,128,128]{2,1,0:T(8,128)S(1)}, f32[3,128,128]{2,1,0:T(8,128)S(1)}, u32[]{:S(2)}, u32[]{:S(2)}) collective-permute-start(f32[3,128,128]{2,1,0:T(8,128)S(1)} %get-tuple-element.7.own), channel_id=1, source_target_pairs={{0,2},{2,0},{4,6},{6,4},{8,10},{10,8},{12,14},{14,12},{1,3},{3,1},... | collective-permute-start | bytes 589832 | tf_op jit(solution)/shard_map/ppermute | solution.py:18
  20.7 4.7 %collective-permute-start.6 = (f32[3,128,128]{2,1,0:T(8,128)S(1)}, f32[3,128,128]{2,1,0:T(8,128)S(1)}, u32[]{:S(2)}, u32[]{:S(2)}) collective-permute-start(f32[3,128,128]{2,1,0:T(8,128)S(1)} %get-tuple-element.7.own), channel_id=1, source_target_pairs={{0,14},{2,4},{4,2},{6,8},{8,6},{10,12},{12,10},{14,0},{1,15},{3,5}... | collective-permute-start | bytes 589832 | tf_op jit(solution)/shard_map/ppermute | solution.py:18
  25.4 1.6 %collective-permute-start.8 = (f32[3,16,128]{2,1,0:T(8,128)S(1)}, f32[3,16,128]{2,1,0:T(8,128)S(1)}, u32[]{:S(2)}, u32[]{:S(2)}) collective-permute-start(f32[3,16,128]{2,1,0:T(8,128)S(1)} %get-tuple-element.8), channel_id=1, source_target_pairs={{0,12},{2,14},{4,8},{6,10},{8,4},{10,6},{12,0},{14,2},{1,13},{3,15... | collective-permute-start | bytes 73736 | tf_op jit(solution)/shard_map/ppermute | solution.py:18
  27.0 2.6 %collective-permute-done.7.far_a = f32[3,16,128]{2,1,0:T(8,128)S(1)} collective-permute-done((f32[3,16,128]{2,1,0:T(8,128)S(1)}, f32[3,16,128]{2,1,0:T(8,128)S(1)}, u32[]{:S(2)}, u32[]{:S(2)}) %collective-permute-start.7) | collective-permute-done | bytes 24608 | tf_op jit(solution)/shard_map/ppermute | solution.py:18
  29.6 0.8 %collective-permute-done.8.far_b = f32[3,16,128]{2,1,0:T(8,128)S(1)} collective-permute-done((f32[3,16,128]{2,1,0:T(8,128)S(1)}, f32[3,16,128]{2,1,0:T(8,128)S(1)}, u32[]{:S(2)}, u32[]{:S(2)}) %collective-permute-start.8) | collective-permute-done | bytes 24608 | tf_op jit(solution)/shard_map/ppermute | solution.py:18
  30.4 1.1 %second_shear.1.own = f32[272,128]{1,0:T(8,128)S(1)} custom-call(s32[8]{0:T(128)S(1)} %stack.46.flags, f32[3,128,128]{2,1,0:T(8,128)S(1)} %get-tuple-element.7.own, f32[3,128,128]{2,1,0:T(8,128)S(1)} %collective-permute-done.5.near_a, f32[3,128,128]{2,1,0:T(8,128)S(1)} %collective-permute-done.6.near_b, f32[3,16,128]{2,1,0:T(8,128)S(1)} %collective-permute-done.7.far_a, ...), custom_call_target="tpu_custom_call" | custom-call | tf_op jit(solution)/shard_map/second_shear/pallas_call | solution.py:204
  32.6 4.6 %all-to-all-start = ((f32[8,8,128]{2,1,0:T(8,128)}), f32[8,8,128]{2,1,0:T(8,128)S(1)}, u32[]{:S(2)}, u32[]{:S(2)}) async-start(f32[8,8,128]{2,1,0:T(8,128)} %broadcast_in_dim.13), calls=%async_computation | async-start | bytes 65536 | tf_op jit(solution)/shard_map/all_to_all | solution.py:225
  37.1 2.7 %collective-permute-start.10 = (f32[272,128]{1,0:T(8,128)S(1)}, f32[272,128]{1,0:T(8,128)S(1)}, u32[]{:S(2)}, u32[]{:S(2)}) collective-permute-start(f32[272,128]{1,0:T(8,128)S(1)} %second_shear.1.own), channel_id=1, source_target_pairs={{0,224},{16,240},{32,64},{48,80},{64,32},{80,48},{96,128},{112,144... | collective-permute-start | bytes 417800 | tf_op jit(solution)/shard_map/ppermute | solution.py:18
  39.8 4.2 %all-to-all-done = f32[8,8,128]{2,1,0:T(8,128)S(1)} async-done(((f32[8,8,128]{2,1,0:T(8,128)}), f32[8,8,128]{2,1,0:T(8,128)S(1)}, u32[]{:S(2)}, u32[]{:S(2)}) %all-to-all-start) | async-done | bytes 32800 | tf_op jit(solution)/shard_map/all_to_all | solution.py:225
  44.7 10.8 %all-to-all-start.1 = ((f32[32,8,128]{2,1,0:T(8,128)}), f32[32,8,128]{2,1,0:T(8,128)S(1)}, u32[]{:S(2)}, u32[]{:S(2)}) async-start(f32[32,8,128]{2,1,0:T(8,128)} %broadcast_in_dim.28), calls=%async_computation.1 | async-start | bytes 262144 | tf_op jit(solution)/shard_map/all_to_all | solution.py:225
  55.5 0.8 %third_shear.1 = (f32[128,128]{1,0:T(8,128)S(1)}, f32[128,128]{1,0:T(8,128)S(1)}) custom-call(s32[8]{0:T(128)S(1)} %stack.46.flags, f32[272,128]{1,0:T(8,128)S(1)} %second_shear.1.own, f32[272,128]{1,0:T(8,128)S(1)} %collective-permute-done.9.near_a, f32[272,128]{1,0:T(8,128)S(1)} %collective-permute-done.10.near_b, s32[1,128]{1,0:T(1,128)S(1)} %get-tuple-element.22.hops, ...), custom_call_target="tpu_custom_call" | custom-call | tf_op jit(solution)/shard_map/third_shear/pallas_call | solution.py:204
  56.6 6.5 %all-to-all-done.1.gathered = f32[32,8,128]{2,1,0:T(8,128)S(1)} async-done(((f32[32,8,128]{2,1,0:T(8,128)}), f32[32,8,128]{2,1,0:T(8,128)S(1)}, u32[]{:S(2)}, u32[]{:S(2)}) %all-to-all-start.1) | async-done | bytes 131104 | tf_op jit(solution)/shard_map/all_to_all | solution.py:225
  63.1 1.6 %exit_wave.1 = f32[2,128]{1,0:T(2,128)} custom-call(s32[8]{0:T(128)S(1)} %stack.46.flags, f32[32,8,128]{2,1,0:T(8,128)S(1)} %all-to-all-done.1.gathered, f32[2,128]{1,0:T(2,128)S(1)} %bitcast.42), custom_call_target="tpu_custom_call" | custom-call | tf_op jit(solution)/shard_map/exit_wave/pallas_call | solution.py:204
  (40 shorter events, 3.6 us)
Async XLA Ops:
  0.6 0.8 %copy-start = (f32[16,8,128]{2,1,0:T(8,128)S(1)}, f32[16,8,128]{2,1,0:T(8,128)}, u32[]{:S(2)}) copy-start(f32[16,8,128]{2,1,0:T(8,128)} %param.11) | copy-start | bytes 196612
  0.7 0.7 %copy-start.2 = (s32[16]{0:T(128)S(1)}, s32[16]{0:T(128)}, u32[]{:S(2)}) copy-start(s32[16]{0:T(128)} %param.12) | copy-start | bytes 196
  3.2 4.2 %collective-permute-start = (f32[144,128]{1,0:T(8,128)S(1)}, f32[144,128]{1,0:T(8,128)S(1)}, u32[]{:S(2)}, u32[]{:S(2)}) collective-permute-start(f32[144,128]{1,0:T(8,128)S(1)} %fusion.1), channel_id=1, source_target_pairs={{0,16},{16,0},{32,48},{48,32},{64,80},{80,64},{96,112},{112,96},{1... | collective-permute-start | bytes 221192 | tf_op jit(solution)/shard_map/ppermute | solution.py:18
  7.7 10.4 %collective-permute-start.1 = (f32[288,128]{1,0:T(8,128)S(1)}, f32[288,128]{1,0:T(8,128)S(1)}, u32[]{:S(2)}, u32[]{:S(2)}) collective-permute-start(f32[288,128]{1,0:T(8,128)S(1)} %pad_maximum_fusion.own), channel_id=1, source_target_pairs={{0,32},{16,48},{32,0},{48,16},{64,96},{80,112},{96,64},{112,80},{1... | collective-permute-start | bytes 442376 | tf_op jit(solution)/shard_map/ppermute | solution.py:18
  7.8 10.3 %collective-permute-start.2 = (f32[288,128]{1,0:T(8,128)S(1)}, f32[288,128]{1,0:T(8,128)S(1)}, u32[]{:S(2)}, u32[]{:S(2)}) collective-permute-start(f32[288,128]{1,0:T(8,128)S(1)} %pad_maximum_fusion.own), channel_id=1, source_target_pairs={{0,224},{16,240},{32,64},{48,80},{64,32},{80,48},{96,128},{112,144... | collective-permute-start | bytes 442376 | tf_op jit(solution)/shard_map/ppermute | solution.py:18
  11.7 4.3 %collective-permute-start.3 = (f32[16,128]{1,0:T(8,128)S(1)}, f32[16,128]{1,0:T(8,128)S(1)}, u32[]{:S(2)}, u32[]{:S(2)}) collective-permute-start(f32[16,128]{1,0:T(8,128)S(1)} %pad_maximum_fusion.5), channel_id=1, source_target_pairs={{0,64},{16,80},{32,96},{48,112},{64,0},{80,16},{96,32},{112,48},{1... | collective-permute-start | bytes 24584 | tf_op jit(solution)/shard_map/ppermute | solution.py:18
  11.7 6.4 %collective-permute-start.4 = (f32[16,128]{1,0:T(8,128)S(1)}, f32[16,128]{1,0:T(8,128)S(1)}, u32[]{:S(2)}, u32[]{:S(2)}) collective-permute-start(f32[16,128]{1,0:T(8,128)S(1)} %pad_maximum_fusion.5), channel_id=1, source_target_pairs={{0,192},{16,208},{32,224},{48,240},{64,128},{80,144},{96,160},{112... | collective-permute-start | bytes 24584 | tf_op jit(solution)/shard_map/ppermute | solution.py:18
  19.0 11.3 %collective-permute-start.5 = (f32[3,128,128]{2,1,0:T(8,128)S(1)}, f32[3,128,128]{2,1,0:T(8,128)S(1)}, u32[]{:S(2)}, u32[]{:S(2)}) collective-permute-start(f32[3,128,128]{2,1,0:T(8,128)S(1)} %get-tuple-element.7.own), channel_id=1, source_target_pairs={{0,2},{2,0},{4,6},{6,4},{8,10},{10,8},{12,14},{14,12},{1,3},{3,1},... | collective-permute-start | bytes 589832 | tf_op jit(solution)/shard_map/ppermute | solution.py:18
  20.7 9.7 %collective-permute-start.6 = (f32[3,128,128]{2,1,0:T(8,128)S(1)}, f32[3,128,128]{2,1,0:T(8,128)S(1)}, u32[]{:S(2)}, u32[]{:S(2)}) collective-permute-start(f32[3,128,128]{2,1,0:T(8,128)S(1)} %get-tuple-element.7.own), channel_id=1, source_target_pairs={{0,14},{2,4},{4,2},{6,8},{8,6},{10,12},{12,10},{14,0},{1,15},{3,5}... | collective-permute-start | bytes 589832 | tf_op jit(solution)/shard_map/ppermute | solution.py:18
  25.4 4.2 %collective-permute-start.7 = (f32[3,16,128]{2,1,0:T(8,128)S(1)}, f32[3,16,128]{2,1,0:T(8,128)S(1)}, u32[]{:S(2)}, u32[]{:S(2)}) collective-permute-start(f32[3,16,128]{2,1,0:T(8,128)S(1)} %get-tuple-element.8), channel_id=1, source_target_pairs={{0,4},{2,6},{4,0},{6,2},{8,12},{10,14},{12,8},{14,10},{1,5},{3,7},... | collective-permute-start | bytes 73736 | tf_op jit(solution)/shard_map/ppermute | solution.py:18
  25.4 5.0 %collective-permute-start.8 = (f32[3,16,128]{2,1,0:T(8,128)S(1)}, f32[3,16,128]{2,1,0:T(8,128)S(1)}, u32[]{:S(2)}, u32[]{:S(2)}) collective-permute-start(f32[3,16,128]{2,1,0:T(8,128)S(1)} %get-tuple-element.8), channel_id=1, source_target_pairs={{0,12},{2,14},{4,8},{6,10},{8,4},{10,6},{12,0},{14,2},{1,13},{3,15... | collective-permute-start | bytes 73736 | tf_op jit(solution)/shard_map/ppermute | solution.py:18
  32.6 4.6 %copy-start.1 = (f32[2,1,128]{2,1,0:T(1,128)S(1)}, f32[2,1,128]{2,1,0:T(1,128)}, u32[]{:S(2)}) copy-start(f32[2,1,128]{2,1,0:T(1,128)} %param.13) | copy-start | bytes 3076
  32.6 11.4 %all-to-all-start = ((f32[8,8,128]{2,1,0:T(8,128)}), f32[8,8,128]{2,1,0:T(8,128)S(1)}, u32[]{:S(2)}, u32[]{:S(2)}) async-start(f32[8,8,128]{2,1,0:T(8,128)} %broadcast_in_dim.13), calls=%async_computation | async-start | bytes 65536 | tf_op jit(solution)/shard_map/all_to_all | solution.py:225
  37.1 18.4 %collective-permute-start.10 = (f32[272,128]{1,0:T(8,128)S(1)}, f32[272,128]{1,0:T(8,128)S(1)}, u32[]{:S(2)}, u32[]{:S(2)}) collective-permute-start(f32[272,128]{1,0:T(8,128)S(1)} %second_shear.1.own), channel_id=1, source_target_pairs={{0,224},{16,240},{32,64},{48,80},{64,32},{80,48},{96,128},{112,144... | collective-permute-start | bytes 417800 | tf_op jit(solution)/shard_map/ppermute | solution.py:18
  39.8 15.7 %collective-permute-start.9 = (f32[272,128]{1,0:T(8,128)S(1)}, f32[272,128]{1,0:T(8,128)S(1)}, u32[]{:S(2)}, u32[]{:S(2)}) collective-permute-start(f32[272,128]{1,0:T(8,128)S(1)} %second_shear.1.own), channel_id=1, source_target_pairs={{0,32},{16,48},{32,0},{48,16},{64,96},{80,112},{96,64},{112,80},{1... | collective-permute-start | bytes 417800 | tf_op jit(solution)/shard_map/ppermute | solution.py:18
  44.7 18.4 %all-to-all-start.1 = ((f32[32,8,128]{2,1,0:T(8,128)}), f32[32,8,128]{2,1,0:T(8,128)S(1)}, u32[]{:S(2)}, u32[]{:S(2)}) async-start(f32[32,8,128]{2,1,0:T(8,128)} %broadcast_in_dim.28), calls=%async_computation.1 | async-start | bytes 262144 | tf_op jit(solution)/shard_map/all_to_all | solution.py:225
  56.3 8.3 %collective-permute-start.11 = (f32[128,128]{1,0:T(8,128)S(1)}, f32[128,128]{1,0:T(8,128)S(1)}, u32[]{:S(2)}, u32[]{:S(2)}) collective-permute-start(f32[128,128]{1,0:T(8,128)S(1)} %get-tuple-element.11), channel_id=1, source_target_pairs={{0,16},{16,0},{32,48},{48,32},{64,80},{80,64},{96,112},{112,96},{1... | collective-permute-start | bytes 196616 | tf_op jit(solution)/shard_map/ppermute | solution.py:18

commit v2 on v1

v2 whole, which is shorter than its diff:
```python
import functools
import math

import jax
import jax.numpy as jnp
from jax import lax
from jax.experimental import pallas as pl
from jax.experimental.pallas import tpu as pltpu
from jax.sharding import PartitionSpec as P

B = 128
SPAN_X = 256
SPAN_Z = 128
VMEM = pltpu.CompilerParams(vmem_limit_bytes=32 * 1024 * 1024)


def permuted(value, axis, target):
    return lax.ppermute(value, axis, [(i, target(i)) for i in range(lax.axis_size(axis))])


def pairings(count):
    return (
        lambda c: c ^ 1,
        lambda c: (c + 1 if c & 1 else c - 1) % count,
        lambda c: c ^ 2,
        lambda c: (c + 2 if c & 2 else c - 2) % count,
    )


def barrel(ref, kept, top, shifts):
    for bit in range(top, -1, -1):
        step = 1 << bit
        rows = kept if bit == top else -(-(kept + step - 1) // 8) * 8
        moved = (shifts & step) != 0
        for start in range(0, rows, 64):
            size = min(64, rows - start)
            here = ref[pl.ds(start, size), :]
            there = ref[pl.ds(start + step, size), :]
            ref[pl.ds(start, size), :] = jnp.where(moved, there, here)


def tap_sum(ref, first_row, size, taps):
    total = None
    for k in range(8):
        term = taps[k : k + 1, :] * ref[pl.ds(first_row + k, size), :]
        total = term if total is None else total + term
    return total


def assemble(ext, at, size, flag, when_set, when_clear, row_set, row_clear):
    ext[pl.ds(at, size), :] = jnp.where(
        flag == 1, when_set[pl.ds(row_set, size), :], when_clear[pl.ds(row_clear, size), :]
    )


def pushed(ref, at, filled, bits, limit, shifts):
    for bit in range(bits):
        step = 1 << bit
        moved = (shifts & step) != 0
        rows = min(limit, -(-(filled + 2 * step - 1) // 8) * 8)
        for start in reversed(range(0, rows, 64)):
            size = min(64, rows - start)
            here = ref[pl.ds(at + start, size), :]
            there = ref[pl.ds(at + start - step, size), :]
            ref[pl.ds(at + start, size), :] = jnp.where(moved, there, here)


def zero(ref, start, stop):
    ref[start:stop, :] = jnp.zeros((stop - start, B), jnp.float32)


def depth_sum_kernel(cells, params, out, padded, spread):
    weights = params[...]
    zero(padded, 0, 8)
    padded[8:264, :] = cells[0:256, :]
    zero(padded, 264, 280)
    zero(spread, 0, B)
    zero(spread, B + 264, B + 512)
    for start in range(0, 264, 88):
        spread[pl.ds(B + start, 88), :] = tap_sum(padded, start + 1, 88, weights)
    shifts = SPAN_X + weights[8:9, :].astype(jnp.int32)
    pushed(spread, B, 264, 7, 512, shifts)
    row = lax.broadcasted_iota(jnp.int32, (8, B), 0)
    sums = lax.dot_general(
        (row == (shifts >> 7)).astype(jnp.float32),
        spread[B : B + 512, :],
        (((1,), (1,)), ((), ())),
        precision=lax.Precision.HIGHEST,
        preferred_element_type=jnp.float32,
    )
    zero(padded, 0, 8)
    for block in range(5):
        for tile in range(4):
            at = block + tile
            if at < 7:
                piece = sums[block : block + 1, tile * B : (tile + 1) * B]
                padded[at : at + 1, :] += piece
    out[...] = padded[0:8, :]


def pack_kernel(
    flags, mine_own, theirs_own, near_a, near_b, far, mine, theirs
):
    core = flags[4]
    for out, channel, own in ((mine, core, mine_own), (theirs, 1 - core, theirs_own)):
        out[0:128, :] = own[...]
        out[128:256, :] = near_a[channel]
        out[256:384, :] = near_b[channel]
        out[384:392, :] = far[channel]


def first_kernel(flags, mine, got, params, out, edges, ext, rows):
    odd, core = flags[0], flags[4]

    def of_core(number, start, size):
        here, there = mine[pl.ds(start, size), :], got[pl.ds(start, size), :]
        return jnp.where(core == number, here, there)

    below = pl.multiple_of(jnp.where(odd == 1, 128, 256), 128)
    above = pl.multiple_of(jnp.where(odd == 1, 256, 128), 128)
    zero(ext, 0, 8)
    ext[8:16, :] = of_core(0, 384, 8)
    for at, start in ((16, below), (272, 0), (528, above)):
        for number in range(2):
            ext[pl.ds(at + number * B, B), :] = of_core(number, start, B)
    ext[784:792, :] = of_core(1, 384, 8)
    zero(ext, 792, 800)
    weights = params[...]
    barrel(ext, 288, 9, SPAN_X - weights[8:9, :].astype(jnp.int32))
    for start in range(0, 256, 64):
        rows[pl.ds(start, 64), :] = tap_sum(ext, start + 13, 64, weights)
    ends = jnp.concatenate([tap_sum(ext, 269, 8, weights), tap_sum(ext, 5, 8, weights)])
    out[256:272, :] = ends
    edges[32:48, :] = ends
    for tile in range(2):
        turned = rows[pl.ds(tile * B, B), :].T
        out[pl.ds(tile * B, B), :] = turned
        edges[pl.ds(8 * tile, 8), :] = turned[0:8, :]
        edges[pl.ds(16 + 8 * tile, 8), :] = turned[120:128, :]


def second_kernel(
    flags, own, near_a, near_b, far_a, far_b, mine, got, out, ext
):
    odd, second_bit, core = flags[2], flags[3], flags[4]
    of_core = lambda number, rows: jnp.where(core == number, mine[rows, :], got[rows, :])
    columns, beside = slice(0, 16), slice(16, 32)
    lane = lax.broadcasted_iota(jnp.int32, (16, B), 1)
    edge = jnp.where(lane < 8, of_core(1, beside), pltpu.roll(of_core(0, beside), 16, 1))
    tiles = [of_core(0, columns), of_core(1, columns), edge]
    for tile in range(3):
        e = ext.at[tile]
        weights = tiles[tile]
        if tile < 2:
            at, edge = tile * B, 8 * tile
            assemble(e, 0, 8, second_bit, far_a, far_b, 16 + edge, 16 + edge)
            assemble(e, 8, 128, odd, near_a, near_b, at, at)
            e[136:264, :] = own[pl.ds(at, B), :]
            assemble(e, 264, 128, odd, near_b, near_a, at, at)
            assemble(e, 392, 8, second_bit, far_b, far_a, edge, edge)
        else:
            below = jnp.where(odd == 1, near_a[256:272, :], near_b[256:272, :])
            above = jnp.where(odd == 1, near_b[256:272, :], near_a[256:272, :])
            far_below = jnp.where(second_bit == 1, far_a[32:48, :], far_b[32:48, :])
            far_above = jnp.where(second_bit == 1, far_b[32:48, :], far_a[32:48, :])
            e[0:8, 0:16] = far_below.T[120:128, :]
            e[8:136, 0:16] = below.T
            e[136:264, 0:16] = own[256:272, :].T
            e[264:392, 0:16] = above.T
            e[392:400, 0:16] = far_above.T[0:8, :]
        barrel(e, 144, 8, SPAN_Z - weights[8:9, :].astype(jnp.int32))
        summed = tap_sum(e, 5, 128, weights).T
        if tile < 2:
            out[pl.ds(tile * B, B), :] = summed
        else:
            out[256:272, :] = summed[0:16, :]

def third_kernel(flags, own, near_a, near_b, params, keep, send, ext):
    odd, core = flags[0], flags[4]
    zero(ext, 0, 8)
    assemble(ext, 8, 8, odd, near_a, near_b, 264, 264)
    assemble(ext, 16, 256, odd, near_a, near_b, 0, 0)
    ext[272:528, :] = own[0:256, :]
    assemble(ext, 528, 264, odd, near_b, near_a, 0, 0)
    zero(ext, 792, 800)
    weights = params[...]
    barrel(ext, 288, 9, SPAN_X - weights[8:9, :].astype(jnp.int32))
    low = tap_sum(ext, 13, B, weights)
    high = tap_sum(ext, 13 + B, B, weights)
    keep[...] = jnp.where(core == 0, low, high)
    send[...] = jnp.where(core == 0, high, low)


def exit_kernel(strength, cells, flags, gathered, illumination, out, acc, loud, proj):
    x_place, y_place = flags[5], flags[6]
    columns = gathered.shape[0] // 2
    row = lax.broadcasted_iota(jnp.int32, (8, B), 0)
    lane = lax.broadcasted_iota(jnp.int32, (columns, B), 1)
    power = None
    for y in range(2):
        for m in range(columns):
            loud[m : m + 1, :] = gathered[2 * m + y, 7:8, :]
        for channel in range(2):
            acc[...] = jnp.zeros(acc.shape, jnp.float32)
            for c in range(columns // 2):
                piece = jnp.where(row < 7, gathered[(2 * c + channel) * 2 + y], 0.0)
                acc[c % 4, pl.ds(2 * c, 8), :] = piece
            whole = (acc[0] + acc[1]) + (acc[2] + acc[3])
            start = whole[0:8, :] + whole[columns:, :]
            acc[0, 0:columns, :] = whole[0:columns, :]
            acc[0, 0:8, :] = start
            acc[0, columns:, :] = start
            below = pltpu.roll(acc[0, 2 : columns + 2, :], B - 4, 1)
            above = pltpu.roll(acc[0, 3 : columns + 3, :], B - 4, 1)
            proj[channel, y] = jnp.where(lane < B - 4, below, above)
        root = jnp.exp((-0.5 * strength) * proj[1, y])
        size = 2.0 * ((loud[...] * root) * root)
        part = size * size
        power = part if power is None else power + part
    power = jnp.sum(power, keepdims=True) / cells
    factor = 2.0 / jnp.sqrt(power + 1e-06)
    angle = strength * proj[0, y_place, pl.ds(x_place, 1), :]
    root = jnp.exp((-0.5 * strength) * proj[1, y_place, pl.ds(x_place, 1), :])
    turn_real, turn_imag = jnp.cos(angle), jnp.sin(angle)
    real, imag = 0.5 * illumination[0:1, :], 0.5 * illumination[1:2, :]
    out[0:1, :] = (((real * turn_real - imag * turn_imag) * root) * root) * factor
    out[1:2, :] = (((real * turn_imag + imag * turn_real) * root) * root) * factor


SMEM_SPEC = pl.BlockSpec(memory_space=pltpu.SMEM)
VMEM_SPEC = pl.BlockSpec(memory_space=pltpu.VMEM)


def call(kernel, name, scalars, arrays, outs, scratch):
    f32 = lambda shape: jax.ShapeDtypeStruct(shape, jnp.float32)
    result = pl.pallas_call(
        kernel,
        out_shape=[f32(shape) for shape in outs],
        in_specs=[SMEM_SPEC] * len(scalars) + [VMEM_SPEC] * len(arrays),
        out_specs=[VMEM_SPEC] * len(outs),
        scratch_shapes=[pltpu.VMEM(shape, jnp.float32) for shape in scratch],
        compiler_params=VMEM,
        name=name,
    )(*scalars, *arrays)
    return result[0] if len(outs) == 1 else result


def half_size(illumination):
    real, imag = jnp.abs(illumination[0]), jnp.abs(illumination[1])
    large, small = jnp.maximum(real, imag), jnp.minimum(real, imag)
    ratio = small / jnp.where(large > 0, large, 1.0)
    return (0.5 * large) * jnp.sqrt(1.0 + ratio * ratio)


def everywhere(value, axes, count):
    copies = jnp.broadcast_to(value[None], (count,) + value.shape)
    return lax.all_to_all(copies, axes, 0, 0, tiled=True)


def local(object_slab, depth_hops, depth_taps, column_hops, column_taps, angle_index, illumination):
    which = angle_index[0]
    gx, gz, gy = lax.axis_index("gx"), lax.axis_index("gz"), lax.axis_index("gy")
    size_x, size_z, size_y = lax.axis_size("gx"), lax.axis_size("gz"), lax.axis_size("gy")
    chip, core = gx // 2, gx % 2
    flags = jnp.stack(
        [chip & 1, (chip >> 1) & 1, gz & 1, (gz >> 1) & 1, core, gx, gy, gy]
    ).astype(jnp.int32)
    padding = jnp.zeros((7, B), jnp.float32)
    params = lambda taps, hops: jnp.concatenate([taps, hops.astype(jnp.float32)[None], padding])
    columns = params(column_taps[which], column_hops[which])
    ring_x = [lambda i, f=f: 2 * f(i // 2) + i % 2 for f in pairings(size_x // 2)]
    ring_z = pairings(size_z)
    outward = lambda steps: lambda i: ((i ^ 1) + (2 * steps if i & 1 else -2 * steps)) % size_x
    slab = object_slab[:, 0]
    near_b, near_a = permuted(slab, "gx", ring_x[1]), permuted(slab, "gx", ring_x[0])
    far = permuted(jnp.where(core == 0, slab[:, 0:8], slab[:, 120:128]), "gx", outward(2))
    beside = permuted(columns, "gx", outward(1))
    swap = lambda i: i ^ 1
    pair = lambda a, b: [jnp.where(core == 0, a, b), jnp.where(core == 0, b, a)]
    mine, theirs = call(
        pack_kernel,
        "pack",
        [flags],
        [*pair(slab[0], slab[1]), near_a, near_b, far],
        [(392, B), (392, B)],
        [],
    )
    theirs, depth_hops, depth_taps = lax.optimization_barrier((theirs, depth_hops, depth_taps))
    hops, taps = depth_hops[which], depth_taps[which]
    first_params, third_params = params(taps[0], hops[0]), params(taps[1], hops[1])
    got = permuted(theirs, "gx", swap)
    first, edges = call(
        first_kernel,
        "first_shear",
        [flags],
        [mine, got, first_params],
        [(272, B), (48, B)],
        [(800, B), (256, B)],
    )
    columns = jnp.concatenate([columns, beside])
    other_columns = permuted(columns, "gx", swap)
    near_a, near_b = permuted(first, "gz", ring_z[0]), permuted(first, "gz", ring_z[1])
    far_a, far_b = permuted(edges, "gz", ring_z[2]), permuted(edges, "gz", ring_z[3])
    second = call(
        second_kernel,
        "second_shear",
        [flags],
        [first, near_a, near_b, far_a, far_b, columns, other_columns],
        [(272, B)],
        [(3, 400, B)],
    )
    near_a, near_b = permuted(second, "gx", ring_x[0]), permuted(second, "gx", ring_x[1])
    sums = call(
        depth_sum_kernel,
        "depth_sum",
        [],
        [second, third_params],
        [(8, B)],
        [(280, B), (B + 512, B)],
    )
    sums = everywhere(sums, "gz", size_z).sum(axis=0)
    sums = jnp.concatenate([sums[:7], half_size(illumination[:, 0])[None]])
    gathered = everywhere(sums, ("gx", "gy"), size_x * size_y)
    keep, send = call(
        third_kernel,
        "third_shear",
        [flags],
        [second, near_a, near_b, third_params],
        [(B, B), (B, B)],
        [(800, B)],
    )
    rotated = jnp.stack(pair(keep, permuted(send, "gx", swap)))
    exit_wave = call(
        functools.partial(
            exit_kernel, 0.5 / math.sqrt(B * size_z), float(size_x * B * size_y)
        ),
        "exit_wave",
        [flags],
        [gathered, illumination[:, 0]],
        [(2, B)],
        [(4, size_x + 8, B), (size_x, B), (2, 2, size_x, B)],
    )
    return (rotated[:, None], exit_wave[:, None])


def solution(mesh):
    return jax.shard_map(
        local,
        mesh=mesh,
        in_specs=(
            P(None, "gy", "gx", "gz"),
            P(None, None, "gz"),
            P(None, None, None, "gz"),
            P(None, "gx"),
            P(None, None, "gx"),
            P(),
            P(None, "gy", "gx"),
        ),
        out_specs=(P(None, "gy", "gx", "gz"), P(None, "gy", "gx")),
        check_vma=False,
    )
```

time: 65.7 us -> 63 us (0.959)
  waiting for transfers between devices: 17.1 us -> 14.3 us
    all_to_all x2, starting transfers between devices: 15.4 us -> 9.14 us  [everywhere(): return lax.all_to_all(copies, axes, 0, 0, tiled=True)]
    ppermute x12 -> x13, starting transfers between devices: 21 us -> 26.8 us  [permuted(): lax.ppermute(value, axis, [(i, target(i)) for i in range(lax.axis_size(ax...]
    ppermute x12 -> x13, waiting for transfers between devices: 6.5 us -> 4.62 us  [permuted(): lax.ppermute(value, axis, [(i, target(i)) for i in range(lax.axis_size(ax...]
    all_to_all x2, waiting for transfers between devices: 10.6 us -> 9.73 us  [everywhere(): return lax.all_to_all(copies, axes, 0, 0, tiled=True)]
    unnamed x0 -> x1, other arithmetic: none -> 0.67 us
    pallas_call x5 -> x6, Pallas kernels: 4.82 us -> 4.95 us  [call(): pl.pallas_call(kernel, out_shape=[f32(shape) for shape in outs], in_specs...]
    select_n x3 -> x2, other arithmetic: 1.63 us -> 1.62 us  [the longest x1 0.88 us: local(): pair = lambda a, b: [jnp.where(core == 0, a, b), jnp.where(core == 0, b, a)]]
  transfers between devices with their start and end apart: 14 -> 15, of which waited for: 7 -> 6; matrix products, arithmetic and copies ran while one was open for 3% -> 6% of each run, Pallas kernels for 4% -> 3%
where the time goes in v2:
time: 63 us; the launch traced here: 62.6 us
  starting transfers between devices  36 us (57%)
  waiting for transfers between devices  14.3 us (23%)
  Pallas kernels  4.95 us (8%)
  local copies, waits for them, and re-layouts  3.44 us (5%)
  other arithmetic  3.05 us (5%)
  between operations  0.88 us (1%)
    ppermute x13, starting transfers between devices, permuted(): lax.ppermute(value, axis, [(i, target(i)) for i in range(lax.axis_size(ax...  26.8 us
    all_to_all x2, waiting for transfers between devices, everywhere(): return lax.all_to_all(copies, axes, 0, 0, tiled=True)  9.73 us
    all_to_all x2, starting transfers between devices, everywhere(): return lax.all_to_all(copies, axes, 0, 0, tiled=True)  9.14 us
    pallas_call x6, Pallas kernels, call(): pl.pallas_call(kernel, out_shape=[f32(shape) for shape in outs], in_specs...  4.95 us
    ppermute x13, waiting for transfers between devices, permuted(): lax.ppermute(value, axis, [(i, target(i)) for i in range(lax.axis_size(ax...  4.62 us
    broadcast_in_dim x2, local copies, waits for them, and re-layouts, everywhere(): copies = jnp.broadcast_to(value[None], (count,) + value.shape)  1.3 us
  transfers between devices with their start and end apart: 15, of which 6 were waited for; matrix products, arithmetic and copies ran while one was open for 6% of the time, Pallas kernels for 3%

profile of v2, /device:TPU:1, one launch (start us, length us, event | category | flops | bytes accessed | tf_op | source)
XLA Modules:
  0.0 62.6 jit_solution(8554804034379321276)
XLA Ops:
  0.6 2.1 %collective-permute-start = (f32[2,128,128]{2,1,0:T(8,128)}, f32[2,128,128]{2,1,0:T(8,128)S(1)}, u32[]{:S(2)}, u32[]{:S(2)}) collective-permute-start(f32[2,128,128]{2,1,0:T(8,128)} %bitcast.49), channel_id=1, source_target_pairs={{0,32},{16,48},{32,0},{48,16},{64,96},{80,112},{96,64},{112,80},{1... | collective-permute-start | bytes 393224 | tf_op jit(solution)/shard_map/ppermute | solution.py:18
  2.8 4.4 %collective-permute-start.1 = (f32[2,128,128]{2,1,0:T(8,128)}, f32[2,128,128]{2,1,0:T(8,128)S(1)}, u32[]{:S(2)}, u32[]{:S(2)}) collective-permute-start(f32[2,128,128]{2,1,0:T(8,128)} %bitcast.50), channel_id=1, source_target_pairs={{0,224},{16,240},{32,64},{48,80},{64,32},{80,48},{96,128},{112,144... | collective-permute-start | bytes 393224 | tf_op jit(solution)/shard_map/ppermute | solution.py:18
  7.2 0.7 %slice_select_fusion = f32[2,8,128]{2,1,0:T(8,128)S(1)} fusion(f32[2,128,128]{2,1,0:T(8,128)} %bitcast.51, pred[]{:T(512)S(6)} %eq.4), kind=kLoop, calls=%fused_computation.9 | loop fusion | flops 2048 | bytes 24577 | tf_op jit(solution)/shard_map/jit(_where)/select_n | solution.py:276
  8.4 0.9 %select_bitcast_fusion.2 = (f32[128,128]{1,0:T(8,128)S(1)}, f32[128,128]{1,0:T(8,128)S(1)}) fusion(f32[2,1,128,128]{3,2,1,0:T(8,128)} %param.7, pred[]{:T(512)S(6)} %eq.4), kind=kLoop, calls=%fused_computation.3 | loop fusion | flops 32768 | bytes 262145 | tf_op jit(solution)/shard_map/jit(_where)/select_n | solution.py:279
  10.1 0.7 %fusion = f32[1,128]{1,0:T(1,128)S(1)} fusion(s32[16,128]{1,0:T(8,128)} %param.10, s32[]{:T(128)S(6)} %select_n.72), kind=kLoop, calls=%fused_computation.17 | loop fusion | flops 128 | bytes 1028 | tf_op jit(solution)/shard_map/convert_element_type | solution.py:269
  10.9 1.7 %collective-permute-done.2.far = f32[2,8,128]{2,1,0:T(8,128)S(1)} collective-permute-done((f32[2,8,128]{2,1,0:T(8,128)S(1)}, f32[2,8,128]{2,1,0:T(8,128)S(1)}, u32[]{:S(2)}, u32[]{:S(2)}) %collective-permute-start.2) | collective-permute-done | bytes 8224 | tf_op jit(solution)/shard_map/ppermute | solution.py:18
  13.1 0.7 %constant_dynamic-slice_fusion.1 = s32[1,2,128]{2,1,0:T(2,128)S(1)} fusion(s32[16,2,128]{2,1,0:T(2,128)} %param.8, s32[]{:T(128)S(6)} %select_n.72), kind=kLoop, calls=%fused_computation.16 | loop fusion | bytes 2052 | tf_op jit(solution)/shard_map/dynamic_slice | solution.py:289
  13.8 3.6 %collective-permute-start.3 = (f32[392,128]{1,0:T(8,128)S(1)}, f32[392,128]{1,0:T(8,128)S(1)}, u32[]{:S(2)}, u32[]{:S(2)}) collective-permute-start(f32[392,128]{1,0:T(8,128)S(1)} %get-tuple-element.13), channel_id=1, source_target_pairs={{0,16},{16,0},{32,48},{48,32},{64,80},{80,64},{96,112},{112,96},{1... | collective-permute-start | bytes 602120 | tf_op jit(solution)/shard_map/ppermute | solution.py:18
  17.5 0.7 %dynamic-slice_bitcast_fusion = (f32[8,128]{1,0:T(8,128)S(1)}, f32[8,128]{1,0:T(8,128)S(1)}) fusion(f32[16,2,8,128]{3,2,1,0:T(8,128)} %param.9, s32[]{:T(128)S(6)} %select_n.72, s32[]{:T(128)S(6)} %add.25), kind=kLoop, calls=%fused_computation.10 | loop fusion | bytes 16392 | tf_op jit(solution)/shard_map/squeeze | solution.py:290
  18.5 0.8 %first_shear.1 = (f32[272,128]{1,0:T(8,128)S(1)}, f32[48,128]{1,0:T(8,128)S(1)}) custom-call(s32[8]{0:T(128)S(1)} %stack.41.flags, f32[392,128]{1,0:T(8,128)S(1)} %get-tuple-element.11.mine, f32[392,128]{1,0:T(8,128)S(1)} %collective-permute-done.3.got, f32[16,128]{1,0:T(8,128)S(1)} %get-tuple-element.32.params), custom_call_target="tpu_custom_call" | custom-call | tf_op jit(solution)/shard_map/first_shear/pallas_call | solution.py:236
  19.4 1.7 %collective-permute-start.4 = (f32[272,128]{1,0:T(8,128)S(1)}, f32[272,128]{1,0:T(8,128)S(1)}, u32[]{:S(2)}, u32[]{:S(2)}) collective-permute-start(f32[272,128]{1,0:T(8,128)S(1)} %get-tuple-element.16.own), channel_id=1, source_target_pairs={{0,2},{2,0},{4,6},{6,4},{8,10},{10,8},{12,14},{14,12},{1,3},{3,1},... | collective-permute-start | bytes 417800 | tf_op jit(solution)/shard_map/ppermute | solution.py:18
  21.1 4.7 %collective-permute-start.5 = (f32[272,128]{1,0:T(8,128)S(1)}, f32[272,128]{1,0:T(8,128)S(1)}, u32[]{:S(2)}, u32[]{:S(2)}) collective-permute-start(f32[272,128]{1,0:T(8,128)S(1)} %get-tuple-element.16.own), channel_id=1, source_target_pairs={{0,14},{2,4},{4,2},{6,8},{8,6},{10,12},{12,10},{14,0},{1,15},{3,5}... | collective-permute-start | bytes 417800 | tf_op jit(solution)/shard_map/ppermute | solution.py:18
  25.8 1.6 %collective-permute-start.7 = (f32[48,128]{1,0:T(8,128)S(1)}, f32[48,128]{1,0:T(8,128)S(1)}, u32[]{:S(2)}, u32[]{:S(2)}) collective-permute-start(f32[48,128]{1,0:T(8,128)S(1)} %get-tuple-element.17), channel_id=1, source_target_pairs={{0,12},{2,14},{4,8},{6,10},{8,4},{10,6},{12,0},{14,2},{1,13},{3,15... | collective-permute-start | bytes 73736 | tf_op jit(solution)/shard_map/ppermute | solution.py:18
  27.4 1.7 %collective-permute-done.8 = f32[16,128]{1,0:T(8,128)S(1)} collective-permute-done((f32[16,128]{1,0:T(8,128)S(1)}, f32[16,128]{1,0:T(8,128)S(1)}, u32[]{:S(2)}, u32[]{:S(2)}) %collective-permute-start.8) | collective-permute-done | bytes 8224 | tf_op jit(solution)/shard_map/ppermute | solution.py:18
  29.1 4.3 %collective-permute-start.9 = (f32[32,128]{1,0:T(8,128)S(1)}, f32[32,128]{1,0:T(8,128)S(1)}, u32[]{:S(2)}, u32[]{:S(2)}) collective-permute-start(f32[32,128]{1,0:T(8,128)S(1)} %pad_maximum_fusion.mine), channel_id=1, source_target_pairs={{0,16},{16,0},{32,48},{48,32},{64,80},{80,64},{96,112},{112,96},{1... | collective-permute-start | bytes 49160 | tf_op jit(solution)/shard_map/ppermute | solution.py:18
  33.4 0.8 %collective-permute-done.9.got = f32[32,128]{1,0:T(8,128)S(1)} collective-permute-done((f32[32,128]{1,0:T(8,128)S(1)}, f32[32,128]{1,0:T(8,128)S(1)}, u32[]{:S(2)}, u32[]{:S(2)}) %collective-permute-start.9) | collective-permute-done | bytes 16416 | tf_op jit(solution)/shard_map/ppermute | solution.py:18
  34.2 0.9 %second_shear.1.own.cells = f32[272,128]{1,0:T(8,128)S(1)} custom-call(s32[8]{0:T(128)S(1)} %stack.41.flags, f32[272,128]{1,0:T(8,128)S(1)} %get-tuple-element.16.own, f32[272,128]{1,0:T(8,128)S(1)} %collective-permute-done.4.near_a, f32[272,128]{1,0:T(8,128)S(1)} %collective-permute-done.5.near_b, f32[48,128]{1,0:T(8,128)S(1)} %collective-permute-done.6.far_a, ...), custom_call_target="tpu_custom_call" | custom-call | tf_op jit(solution)/shard_map/second_shear/pallas_call | solution.py:236
  36.3 3.5 %all-to-all-start = ((f32[8,8,128]{2,1,0:T(8,128)}), f32[8,8,128]{2,1,0:T(8,128)S(1)}, u32[]{:S(2)}, u32[]{:S(2)}) async-start(f32[8,8,128]{2,1,0:T(8,128)} %broadcast_in_dim.16), calls=%async_computation | async-start | bytes 65536 | tf_op jit(solution)/shard_map/all_to_all | solution.py:257
  39.9 3.5 %collective-permute-start.11 = (f32[272,128]{1,0:T(8,128)S(1)}, f32[272,128]{1,0:T(8,128)S(1)}, u32[]{:S(2)}, u32[]{:S(2)}) collective-permute-start(f32[272,128]{1,0:T(8,128)S(1)} %second_shear.1.own.cells), channel_id=1, source_target_pairs={{0,224},{16,240},{32,64},{48,80},{64,32},{80,48},{96,128},{112,144... | collective-permute-start | bytes 417800 | tf_op jit(solution)/shard_map/ppermute | solution.py:18
  43.4 3.3 %all-to-all-done = f32[8,8,128]{2,1,0:T(8,128)S(1)} async-done(((f32[8,8,128]{2,1,0:T(8,128)}), f32[8,8,128]{2,1,0:T(8,128)S(1)}, u32[]{:S(2)}, u32[]{:S(2)}) %all-to-all-start) | async-done | bytes 32800 | tf_op jit(solution)/shard_map/all_to_all | solution.py:257
  47.3 5.7 %all-to-all-start.1 = ((f32[32,8,128]{2,1,0:T(8,128)}), f32[32,8,128]{2,1,0:T(8,128)S(1)}, u32[]{:S(2)}, u32[]{:S(2)}) async-start(f32[32,8,128]{2,1,0:T(8,128)} %broadcast_in_dim.33), calls=%async_computation.1 | async-start | bytes 262144 | tf_op jit(solution)/shard_map/all_to_all | solution.py:257
  53.0 0.8 %third_shear.1 = (f32[128,128]{1,0:T(8,128)S(1)}, f32[128,128]{1,0:T(8,128)S(1)}) custom-call(s32[8]{0:T(128)S(1)} %stack.41.flags, f32[272,128]{1,0:T(8,128)S(1)} %second_shear.1.own.cells, f32[272,128]{1,0:T(8,128)S(1)} %collective-permute-done.10.near_a, f32[272,128]{1,0:T(8,128)S(1)} %collective-permute-done.11.near_b, ...), custom_call_target="tpu_custom_call" | custom-call | tf_op jit(solution)/shard_map/third_shear/pallas_call | solution.py:236
  54.1 6.5 %all-to-all-done.1.gathered = f32[32,8,128]{2,1,0:T(8,128)S(1)} async-done(((f32[32,8,128]{2,1,0:T(8,128)}), f32[32,8,128]{2,1,0:T(8,128)S(1)}, u32[]{:S(2)}, u32[]{:S(2)}) %all-to-all-start.1) | async-done | bytes 131104 | tf_op jit(solution)/shard_map/all_to_all | solution.py:257
  60.6 1.4 %exit_wave.1 = f32[2,128]{1,0:T(2,128)} custom-call(s32[8]{0:T(128)S(1)} %stack.41.flags, f32[32,8,128]{2,1,0:T(8,128)S(1)} %all-to-all-done.1.gathered, f32[2,128]{1,0:T(2,128)S(1)} %bitcast.48), custom_call_target="tpu_custom_call" | custom-call | tf_op jit(solution)/shard_map/exit_wave/pallas_call | solution.py:236
  (36 shorter events, 5.1 us)
Async XLA Ops:
  0.6 9.4 %copy-start = (f32[16,8,128]{2,1,0:T(8,128)S(1)}, f32[16,8,128]{2,1,0:T(8,128)}, u32[]{:S(2)}) copy-start(f32[16,8,128]{2,1,0:T(8,128)} %param.11) | copy-start | bytes 196612
  0.6 11.9 %collective-permute-start = (f32[2,128,128]{2,1,0:T(8,128)}, f32[2,128,128]{2,1,0:T(8,128)S(1)}, u32[]{:S(2)}, u32[]{:S(2)}) collective-permute-start(f32[2,128,128]{2,1,0:T(8,128)} %bitcast.49), channel_id=1, source_target_pairs={{0,32},{16,48},{32,0},{48,16},{64,96},{80,112},{96,64},{112,80},{1... | collective-permute-start | bytes 393224 | tf_op jit(solution)/shard_map/ppermute | solution.py:18
  2.8 9.8 %collective-permute-start.1 = (f32[2,128,128]{2,1,0:T(8,128)}, f32[2,128,128]{2,1,0:T(8,128)S(1)}, u32[]{:S(2)}, u32[]{:S(2)}) collective-permute-start(f32[2,128,128]{2,1,0:T(8,128)} %bitcast.50), channel_id=1, source_target_pairs={{0,224},{16,240},{32,64},{48,80},{64,32},{80,48},{96,128},{112,144... | collective-permute-start | bytes 393224 | tf_op jit(solution)/shard_map/ppermute | solution.py:18
  8.0 4.6 %collective-permute-start.2 = (f32[2,8,128]{2,1,0:T(8,128)S(1)}, f32[2,8,128]{2,1,0:T(8,128)S(1)}, u32[]{:S(2)}, u32[]{:S(2)}) collective-permute-start(f32[2,8,128]{2,1,0:T(8,128)S(1)} %slice_select_fusion), channel_id=1, source_target_pairs={{0,208},{16,64},{32,240},{48,96},{64,16},{80,128},{96,48},{112,160... | collective-permute-start | bytes 24584 | tf_op jit(solution)/shard_map/ppermute | solution.py:18
  9.3 0.7 %copy-start.2 = (s32[16]{0:T(128)S(1)}, s32[16]{0:T(128)}, u32[]{:S(2)}) copy-start(s32[16]{0:T(128)} %param.12) | copy-start | bytes 196
  13.8 4.7 %collective-permute-start.3 = (f32[392,128]{1,0:T(8,128)S(1)}, f32[392,128]{1,0:T(8,128)S(1)}, u32[]{:S(2)}, u32[]{:S(2)}) collective-permute-start(f32[392,128]{1,0:T(8,128)S(1)} %get-tuple-element.13), channel_id=1, source_target_pairs={{0,16},{16,0},{32,48},{48,32},{64,80},{80,64},{96,112},{112,96},{1... | collective-permute-start | bytes 602120 | tf_op jit(solution)/shard_map/ppermute | solution.py:18
  19.4 14.9 %collective-permute-start.4 = (f32[272,128]{1,0:T(8,128)S(1)}, f32[272,128]{1,0:T(8,128)S(1)}, u32[]{:S(2)}, u32[]{:S(2)}) collective-permute-start(f32[272,128]{1,0:T(8,128)S(1)} %get-tuple-element.16.own), channel_id=1, source_target_pairs={{0,2},{2,0},{4,6},{6,4},{8,10},{10,8},{12,14},{14,12},{1,3},{3,1},... | collective-permute-start | bytes 417800 | tf_op jit(solution)/shard_map/ppermute | solution.py:18
  21.1 13.2 %collective-permute-start.5 = (f32[272,128]{1,0:T(8,128)S(1)}, f32[272,128]{1,0:T(8,128)S(1)}, u32[]{:S(2)}, u32[]{:S(2)}) collective-permute-start(f32[272,128]{1,0:T(8,128)S(1)} %get-tuple-element.16.own), channel_id=1, source_target_pairs={{0,14},{2,4},{4,2},{6,8},{8,6},{10,12},{12,10},{14,0},{1,15},{3,5}... | collective-permute-start | bytes 417800 | tf_op jit(solution)/shard_map/ppermute | solution.py:18
  25.8 3.4 %collective-permute-start.8 = (f32[16,128]{1,0:T(8,128)S(1)}, f32[16,128]{1,0:T(8,128)S(1)}, u32[]{:S(2)}, u32[]{:S(2)}) collective-permute-start(f32[16,128]{1,0:T(8,128)S(1)} %get-tuple-element.31), channel_id=1, source_target_pairs={{0,240},{16,32},{32,16},{48,64},{64,48},{80,96},{96,80},{112,128},... | collective-permute-start | bytes 24584 | tf_op jit(solution)/shard_map/ppermute | solution.py:18
  25.8 8.5 %collective-permute-start.6 = (f32[48,128]{1,0:T(8,128)S(1)}, f32[48,128]{1,0:T(8,128)S(1)}, u32[]{:S(2)}, u32[]{:S(2)}) collective-permute-start(f32[48,128]{1,0:T(8,128)S(1)} %get-tuple-element.17), channel_id=1, source_target_pairs={{0,4},{2,6},{4,0},{6,2},{8,12},{10,14},{12,8},{14,10},{1,5},{3,7},... | collective-permute-start | bytes 73736 | tf_op jit(solution)/shard_map/ppermute | solution.py:18
  25.8 8.5 %collective-permute-start.7 = (f32[48,128]{1,0:T(8,128)S(1)}, f32[48,128]{1,0:T(8,128)S(1)}, u32[]{:S(2)}, u32[]{:S(2)}) collective-permute-start(f32[48,128]{1,0:T(8,128)S(1)} %get-tuple-element.17), channel_id=1, source_target_pairs={{0,12},{2,14},{4,8},{6,10},{8,4},{10,6},{12,0},{14,2},{1,13},{3,15... | collective-permute-start | bytes 73736 | tf_op jit(solution)/shard_map/ppermute | solution.py:18
  29.1 5.1 %collective-permute-start.9 = (f32[32,128]{1,0:T(8,128)S(1)}, f32[32,128]{1,0:T(8,128)S(1)}, u32[]{:S(2)}, u32[]{:S(2)}) collective-permute-start(f32[32,128]{1,0:T(8,128)S(1)} %pad_maximum_fusion.mine), channel_id=1, source_target_pairs={{0,16},{16,0},{32,48},{48,32},{64,80},{80,64},{96,112},{112,96},{1... | collective-permute-start | bytes 49160 | tf_op jit(solution)/shard_map/ppermute | solution.py:18
  36.3 3.5 %copy-start.1 = (f32[2,1,128]{2,1,0:T(1,128)S(1)}, f32[2,1,128]{2,1,0:T(1,128)}, u32[]{:S(2)}) copy-start(f32[2,1,128]{2,1,0:T(1,128)} %param.13) | copy-start | bytes 3076
  36.3 10.3 %all-to-all-start = ((f32[8,8,128]{2,1,0:T(8,128)}), f32[8,8,128]{2,1,0:T(8,128)S(1)}, u32[]{:S(2)}, u32[]{:S(2)}) async-start(f32[8,8,128]{2,1,0:T(8,128)} %broadcast_in_dim.16), calls=%async_computation | async-start | bytes 65536 | tf_op jit(solution)/shard_map/all_to_all | solution.py:257
  39.8 13.2 %collective-permute-start.10 = (f32[272,128]{1,0:T(8,128)S(1)}, f32[272,128]{1,0:T(8,128)S(1)}, u32[]{:S(2)}, u32[]{:S(2)}) collective-permute-start(f32[272,128]{1,0:T(8,128)S(1)} %second_shear.1.own.cells), channel_id=1, source_target_pairs={{0,32},{16,48},{32,0},{48,16},{64,96},{80,112},{96,64},{112,80},{1... | collective-permute-start | bytes 417800 | tf_op jit(solution)/shard_map/ppermute | solution.py:18
  39.9 13.1 %collective-permute-start.11 = (f32[272,128]{1,0:T(8,128)S(1)}, f32[272,128]{1,0:T(8,128)S(1)}, u32[]{:S(2)}, u32[]{:S(2)}) collective-permute-start(f32[272,128]{1,0:T(8,128)S(1)} %second_shear.1.own.cells), channel_id=1, source_target_pairs={{0,224},{16,240},{32,64},{48,80},{64,32},{80,48},{96,128},{112,144... | collective-permute-start | bytes 417800 | tf_op jit(solution)/shard_map/ppermute | solution.py:18
  47.3 13.2 %all-to-all-start.1 = ((f32[32,8,128]{2,1,0:T(8,128)}), f32[32,8,128]{2,1,0:T(8,128)S(1)}, u32[]{:S(2)}, u32[]{:S(2)}) async-start(f32[32,8,128]{2,1,0:T(8,128)} %broadcast_in_dim.33), calls=%async_computation.1 | async-start | bytes 262144 | tf_op jit(solution)/shard_map/all_to_all | solution.py:257
  53.8 8.2 %collective-permute-start.12 = (f32[128,128]{1,0:T(8,128)S(1)}, f32[128,128]{1,0:T(8,128)S(1)}, u32[]{:S(2)}, u32[]{:S(2)}) collective-permute-start(f32[128,128]{1,0:T(8,128)S(1)} %get-tuple-element.19), channel_id=1, source_target_pairs={{0,16},{16,0},{32,48},{48,32},{64,80},{80,64},{96,112},{112,96},{1... | collective-permute-start | bytes 196616 | tf_op jit(solution)/shard_map/ppermute | solution.py:18

commit v3 on v2

--- a/solution.py
+++ b/solution.py
@@ -99,28 +99,26 @@
 
 
 def pack_kernel(
-    flags, mine_own, theirs_own, near_a, near_b, far, mine, theirs
+    flags, mine_own, theirs_own, below, above, far, mine, theirs
 ):
     core = flags[4]
     for out, channel, own in ((mine, core, mine_own), (theirs, 1 - core, theirs_own)):
         out[0:128, :] = own[...]
-        out[128:256, :] = near_a[channel]
-        out[256:384, :] = near_b[channel]
+        out[128:256, :] = below[channel]
+        out[256:384, :] = above[channel]
         out[384:392, :] = far[channel]
 
 
 def first_kernel(flags, mine, got, params, out, edges, ext, rows):
-    odd, core = flags[0], flags[4]
+    core = flags[4]
 
     def of_core(number, start, size):
         here, there = mine[pl.ds(start, size), :], got[pl.ds(start, size), :]
         return jnp.where(core == number, here, there)
 
-    below = pl.multiple_of(jnp.where(odd == 1, 128, 256), 128)
-    above = pl.multiple_of(jnp.where(odd == 1, 256, 128), 128)
     zero(ext, 0, 8)
     ext[8:16, :] = of_core(0, 384, 8)
-    for at, start in ((16, below), (272, 0), (528, above)):
+    for at, start in ((16, 128), (272, 0), (528, 256)):
         for number in range(2):
             ext[pl.ds(at + number * B, B), :] = of_core(number, start, B)
     ext[784:792, :] = of_core(1, 384, 8)
@@ -272,7 +270,8 @@
     ring_z = pairings(size_z)
     outward = lambda steps: lambda i: ((i ^ 1) + (2 * steps if i & 1 else -2 * steps)) % size_x
     slab = object_slab[:, 0]
-    near_b, near_a = permuted(slab, "gx", ring_x[1]), permuted(slab, "gx", ring_x[0])
+    below = permuted(slab, "gx", lambda i: (i + 2) % size_x)
+    above = permuted(slab, "gx", lambda i: (i - 2) % size_x)
     far = permuted(jnp.where(core == 0, slab[:, 0:8], slab[:, 120:128]), "gx", outward(2))
     beside = permuted(columns, "gx", outward(1))
     swap = lambda i: i ^ 1
@@ -281,11 +280,10 @@
         pack_kernel,
         "pack",
         [flags],
-        [*pair(slab[0], slab[1]), near_a, near_b, far],
+        [*pair(slab[0], slab[1]), below, above, far],
         [(392, B), (392, B)],
         [],
     )
-    theirs, depth_hops, depth_taps = lax.optimization_barrier((theirs, depth_hops, depth_taps))
     hops, taps = depth_hops[which], depth_taps[which]
     first_params, third_params = params(taps[0], hops[0]), params(taps[1], hops[1])
     got = permuted(theirs, "gx", swap)

time: 63 us -> 62.7 us (level)
    ppermute x13, starting transfers between devices: 26.8 us -> 25.7 us  [permuted(): lax.ppermute(value, axis, [(i, target(i)) for i in range(lax.axis_size(ax...]
    all_to_all x2, starting transfers between devices: 9.14 us -> 9.99 us  [everywhere(): return lax.all_to_all(copies, axes, 0, 0, tiled=True)]
  transfers between devices with their start and end apart: 15 -> 15, of which waited for: 6 -> 6; matrix products, arithmetic and copies ran while one was open for 6% -> 7% of each run, Pallas kernels for 3% -> 3%
where the time goes in v3:
time: 62.7 us; the launch traced here: 62.3 us
  starting transfers between devices  35.7 us (57%)
  waiting for transfers between devices  14.3 us (23%)
  Pallas kernels  4.95 us (8%)
  local copies, waits for them, and re-layouts  3.44 us (5%)
  other arithmetic  3.04 us (5%)
  between operations  0.87 us (1%)
    ppermute x13, starting transfers between devices, permuted(): lax.ppermute(value, axis, [(i, target(i)) for i in range(lax.axis_size(ax...  25.7 us
    all_to_all x2, starting transfers between devices, everywhere(): return lax.all_to_all(copies, axes, 0, 0, tiled=True)  9.99 us
    all_to_all x2, waiting for transfers between devices, everywhere(): return lax.all_to_all(copies, axes, 0, 0, tiled=True)  9.77 us
    pallas_call x6, Pallas kernels, call(): pl.pallas_call(kernel, out_shape=[f32(shape) for shape in outs], in_specs...  4.95 us
    ppermute x13, waiting for transfers between devices, permuted(): lax.ppermute(value, axis, [(i, target(i)) for i in range(lax.axis_size(ax...  4.57 us
    broadcast_in_dim x2, local copies, waits for them, and re-layouts, everywhere(): copies = jnp.broadcast_to(value[None], (count,) + value.shape)  1.3 us
  transfers between devices with their start and end apart: 15, of which 6 were waited for; matrix products, arithmetic and copies ran while one was open for 7% of the time, Pallas kernels for 3%

profile of v3, /device:TPU:1, one launch (start us, length us, event | category | flops | bytes accessed | tf_op | source)
XLA Modules:
  0.0 62.3 jit_solution(15848271027258548953)
XLA Ops:
  0.6 2.1 %collective-permute-start = (f32[2,128,128]{2,1,0:T(8,128)}, f32[2,128,128]{2,1,0:T(8,128)S(1)}, u32[]{:S(2)}, u32[]{:S(2)}) collective-permute-start(f32[2,128,128]{2,1,0:T(8,128)} %bitcast.49), channel_id=1, source_target_pairs={{0,32},{16,48},{32,64},{48,80},{64,96},{80,112},{96,128},{112,144}... | collective-permute-start | bytes 393224 | tf_op jit(solution)/shard_map/ppermute | solution.py:18
  2.8 4.0 %collective-permute-start.1 = (f32[2,128,128]{2,1,0:T(8,128)}, f32[2,128,128]{2,1,0:T(8,128)S(1)}, u32[]{:S(2)}, u32[]{:S(2)}) collective-permute-start(f32[2,128,128]{2,1,0:T(8,128)} %bitcast.50), channel_id=1, source_target_pairs={{0,224},{16,240},{32,0},{48,16},{64,32},{80,48},{96,64},{112,80},{... | collective-permute-start | bytes 393224 | tf_op jit(solution)/shard_map/ppermute | solution.py:18
  6.8 0.7 %slice_select_fusion = f32[2,8,128]{2,1,0:T(8,128)S(1)} fusion(f32[2,128,128]{2,1,0:T(8,128)} %bitcast.51, pred[]{:T(512)S(6)} %eq.4), kind=kLoop, calls=%fused_computation.9 | loop fusion | flops 2048 | bytes 24577 | tf_op jit(solution)/shard_map/jit(_where)/select_n | solution.py:275
  7.6 0.9 %select_bitcast_fusion.2 = (f32[128,128]{1,0:T(8,128)S(1)}, f32[128,128]{1,0:T(8,128)S(1)}) fusion(f32[2,1,128,128]{3,2,1,0:T(8,128)} %param.7, pred[]{:T(512)S(6)} %eq.4), kind=kLoop, calls=%fused_computation.3 | loop fusion | flops 32768 | bytes 262145 | tf_op jit(solution)/shard_map/jit(_where)/select_n | solution.py:278
  9.3 0.7 %constant_dynamic-slice_fusion.1 = s32[1,2,128]{2,1,0:T(2,128)S(1)} fusion(s32[16,2,128]{2,1,0:T(2,128)} %param.8, s32[]{:T(128)S(6)} %select_n.72), kind=kLoop, calls=%fused_computation.16 | loop fusion | bytes 2052 | tf_op jit(solution)/shard_map/dynamic_slice | solution.py:287
  10.0 0.7 %dynamic-slice_bitcast_fusion = (f32[8,128]{1,0:T(8,128)S(1)}, f32[8,128]{1,0:T(8,128)S(1)}) fusion(f32[16,2,8,128]{3,2,1,0:T(8,128)} %param.9, s32[]{:T(128)S(6)} %select_n.72, s32[]{:T(128)S(6)} %add.25), kind=kLoop, calls=%fused_computation.10 | loop fusion | bytes 16392 | tf_op jit(solution)/shard_map/squeeze | solution.py:288
  10.8 1.6 %collective-permute-done.2.far = f32[2,8,128]{2,1,0:T(8,128)S(1)} collective-permute-done((f32[2,8,128]{2,1,0:T(8,128)S(1)}, f32[2,8,128]{2,1,0:T(8,128)S(1)}, u32[]{:S(2)}, u32[]{:S(2)}) %collective-permute-start.2) | collective-permute-done | bytes 8224 | tf_op jit(solution)/shard_map/ppermute | solution.py:18
  12.9 5.0 %collective-permute-start.3 = (f32[392,128]{1,0:T(8,128)S(1)}, f32[392,128]{1,0:T(8,128)S(1)}, u32[]{:S(2)}, u32[]{:S(2)}) collective-permute-start(f32[392,128]{1,0:T(8,128)S(1)} %get-tuple-element.9), channel_id=1, source_target_pairs={{0,16},{16,0},{32,48},{48,32},{64,80},{80,64},{96,112},{112,96},{1... | collective-permute-start | bytes 602120 | tf_op jit(solution)/shard_map/ppermute | solution.py:18
  18.0 0.7 %fusion = f32[1,128]{1,0:T(1,128)S(1)} fusion(s32[16,128]{1,0:T(8,128)} %param.10, s32[]{:T(128)S(6)} %select_n.72), kind=kLoop, calls=%fused_computation.17 | loop fusion | flops 128 | bytes 1028 | tf_op jit(solution)/shard_map/convert_element_type | solution.py:267
  19.1 0.8 %first_shear.1 = (f32[272,128]{1,0:T(8,128)S(1)}, f32[48,128]{1,0:T(8,128)S(1)}) custom-call(s32[8]{0:T(128)S(1)} %stack.41.flags, f32[392,128]{1,0:T(8,128)S(1)} %get-tuple-element.8.mine, f32[392,128]{1,0:T(8,128)S(1)} %collective-permute-done.3.got, f32[16,128]{1,0:T(8,128)S(1)} %get-tuple-element.26.params), custom_call_target="tpu_custom_call" | custom-call | tf_op jit(solution)/shard_map/first_shear/pallas_call | solution.py:234
  20.0 4.6 %collective-permute-start.5 = (f32[272,128]{1,0:T(8,128)S(1)}, f32[272,128]{1,0:T(8,128)S(1)}, u32[]{:S(2)}, u32[]{:S(2)}) collective-permute-start(f32[272,128]{1,0:T(8,128)S(1)} %get-tuple-element.10.own), channel_id=1, source_target_pairs={{0,14},{2,4},{4,2},{6,8},{8,6},{10,12},{12,10},{14,0},{1,15},{3,5}... | collective-permute-start | bytes 417800 | tf_op jit(solution)/shard_map/ppermute | solution.py:18
  24.6 1.6 %collective-permute-start.7 = (f32[48,128]{1,0:T(8,128)S(1)}, f32[48,128]{1,0:T(8,128)S(1)}, u32[]{:S(2)}, u32[]{:S(2)}) collective-permute-start(f32[48,128]{1,0:T(8,128)S(1)} %get-tuple-element.11), channel_id=1, source_target_pairs={{0,12},{2,14},{4,8},{6,10},{8,4},{10,6},{12,0},{14,2},{1,13},{3,15... | collective-permute-start | bytes 73736 | tf_op jit(solution)/shard_map/ppermute | solution.py:18
  26.2 1.7 %collective-permute-done.8 = f32[16,128]{1,0:T(8,128)S(1)} collective-permute-done((f32[16,128]{1,0:T(8,128)S(1)}, f32[16,128]{1,0:T(8,128)S(1)}, u32[]{:S(2)}, u32[]{:S(2)}) %collective-permute-start.8) | collective-permute-done | bytes 8224 | tf_op jit(solution)/shard_map/ppermute | solution.py:18
  27.9 4.3 %collective-permute-start.9 = (f32[32,128]{1,0:T(8,128)S(1)}, f32[32,128]{1,0:T(8,128)S(1)}, u32[]{:S(2)}, u32[]{:S(2)}) collective-permute-start(f32[32,128]{1,0:T(8,128)S(1)} %pad_maximum_fusion.mine), channel_id=1, source_target_pairs={{0,16},{16,0},{32,48},{48,32},{64,80},{80,64},{96,112},{112,96},{1... | collective-permute-start | bytes 49160 | tf_op jit(solution)/shard_map/ppermute | solution.py:18
  32.2 0.8 %collective-permute-done.9.got = f32[32,128]{1,0:T(8,128)S(1)} collective-permute-done((f32[32,128]{1,0:T(8,128)S(1)}, f32[32,128]{1,0:T(8,128)S(1)}, u32[]{:S(2)}, u32[]{:S(2)}) %collective-permute-start.9) | collective-permute-done | bytes 16416 | tf_op jit(solution)/shard_map/ppermute | solution.py:18
  33.1 0.9 %second_shear.1.own.cells = f32[272,128]{1,0:T(8,128)S(1)} custom-call(s32[8]{0:T(128)S(1)} %stack.41.flags, f32[272,128]{1,0:T(8,128)S(1)} %get-tuple-element.10.own, f32[272,128]{1,0:T(8,128)S(1)} %collective-permute-done.4.near_a, f32[272,128]{1,0:T(8,128)S(1)} %collective-permute-done.5.near_b, f32[48,128]{1,0:T(8,128)S(1)} %collective-permute-done.6.far_a, ...), custom_call_target="tpu_custom_call" | custom-call | tf_op jit(solution)/shard_map/second_shear/pallas_call | solution.py:234
  35.1 3.5 %all-to-all-start = ((f32[8,8,128]{2,1,0:T(8,128)}), f32[8,8,128]{2,1,0:T(8,128)S(1)}, u32[]{:S(2)}, u32[]{:S(2)}) async-start(f32[8,8,128]{2,1,0:T(8,128)} %broadcast_in_dim.16), calls=%async_computation | async-start | bytes 65536 | tf_op jit(solution)/shard_map/all_to_all | solution.py:255
  38.7 3.5 %collective-permute-start.11 = (f32[272,128]{1,0:T(8,128)S(1)}, f32[272,128]{1,0:T(8,128)S(1)}, u32[]{:S(2)}, u32[]{:S(2)}) collective-permute-start(f32[272,128]{1,0:T(8,128)S(1)} %second_shear.1.own.cells), channel_id=1, source_target_pairs={{0,224},{16,240},{32,64},{48,80},{64,32},{80,48},{96,128},{112,144... | collective-permute-start | bytes 417800 | tf_op jit(solution)/shard_map/ppermute | solution.py:18
  42.2 3.3 %all-to-all-done = f32[8,8,128]{2,1,0:T(8,128)S(1)} async-done(((f32[8,8,128]{2,1,0:T(8,128)}), f32[8,8,128]{2,1,0:T(8,128)S(1)}, u32[]{:S(2)}, u32[]{:S(2)}) %all-to-all-start) | async-done | bytes 32800 | tf_op jit(solution)/shard_map/all_to_all | solution.py:255
  45.5 0.7 %broadcast_in_dim.33 = f32[32,8,128]{2,1,0:T(8,128)} broadcast(f32[8,128]{1,0:T(8,128)S(1)} %pad_maximum_fusion.4), dimensions={1,2} | broadcast | bytes 135168 | tf_op jit(solution)/shard_map/broadcast_in_dim | solution.py:254
  46.2 6.5 %all-to-all-start.1 = ((f32[32,8,128]{2,1,0:T(8,128)}), f32[32,8,128]{2,1,0:T(8,128)S(1)}, u32[]{:S(2)}, u32[]{:S(2)}) async-start(f32[32,8,128]{2,1,0:T(8,128)} %broadcast_in_dim.33), calls=%async_computation.1 | async-start | bytes 262144 | tf_op jit(solution)/shard_map/all_to_all | solution.py:255
  52.7 0.8 %third_shear.1 = (f32[128,128]{1,0:T(8,128)S(1)}, f32[128,128]{1,0:T(8,128)S(1)}) custom-call(s32[8]{0:T(128)S(1)} %stack.41.flags, f32[272,128]{1,0:T(8,128)S(1)} %second_shear.1.own.cells, f32[272,128]{1,0:T(8,128)S(1)} %collective-permute-done.10.near_a, f32[272,128]{1,0:T(8,128)S(1)} %collective-permute-done.11.near_b, ...), custom_call_target="tpu_custom_call" | custom-call | tf_op jit(solution)/shard_map/third_shear/pallas_call | solution.py:234
  53.8 6.5 %all-to-all-done.1.gathered = f32[32,8,128]{2,1,0:T(8,128)S(1)} async-done(((f32[32,8,128]{2,1,0:T(8,128)}), f32[32,8,128]{2,1,0:T(8,128)S(1)}, u32[]{:S(2)}, u32[]{:S(2)}) %all-to-all-start.1) | async-done | bytes 131104 | tf_op jit(solution)/shard_map/all_to_all | solution.py:255
  60.3 1.4 %exit_wave.1 = f32[2,128]{1,0:T(2,128)} custom-call(s32[8]{0:T(128)S(1)} %stack.41.flags, f32[32,8,128]{2,1,0:T(8,128)S(1)} %all-to-all-done.1.gathered, f32[2,128]{1,0:T(2,128)S(1)} %bitcast.48), custom_call_target="tpu_custom_call" | custom-call | tf_op jit(solution)/shard_map/exit_wave/pallas_call | solution.py:234
  (36 shorter events, 4.2 us)
Async XLA Ops:
  0.6 10.0 %copy-start = (f32[16,8,128]{2,1,0:T(8,128)S(1)}, f32[16,8,128]{2,1,0:T(8,128)}, u32[]{:S(2)}) copy-start(f32[16,8,128]{2,1,0:T(8,128)} %param.11) | copy-start | bytes 196612
  0.6 11.7 %collective-permute-start = (f32[2,128,128]{2,1,0:T(8,128)}, f32[2,128,128]{2,1,0:T(8,128)S(1)}, u32[]{:S(2)}, u32[]{:S(2)}) collective-permute-start(f32[2,128,128]{2,1,0:T(8,128)} %bitcast.49), channel_id=1, source_target_pairs={{0,32},{16,48},{32,64},{48,80},{64,96},{80,112},{96,128},{112,144}... | collective-permute-start | bytes 393224 | tf_op jit(solution)/shard_map/ppermute | solution.py:18
  2.8 9.6 %collective-permute-start.1 = (f32[2,128,128]{2,1,0:T(8,128)}, f32[2,128,128]{2,1,0:T(8,128)S(1)}, u32[]{:S(2)}, u32[]{:S(2)}) collective-permute-start(f32[2,128,128]{2,1,0:T(8,128)} %bitcast.50), channel_id=1, source_target_pairs={{0,224},{16,240},{32,0},{48,16},{64,32},{80,48},{96,64},{112,80},{... | collective-permute-start | bytes 393224 | tf_op jit(solution)/shard_map/ppermute | solution.py:18
  7.5 4.9 %collective-permute-start.2 = (f32[2,8,128]{2,1,0:T(8,128)S(1)}, f32[2,8,128]{2,1,0:T(8,128)S(1)}, u32[]{:S(2)}, u32[]{:S(2)}) collective-permute-start(f32[2,8,128]{2,1,0:T(8,128)S(1)} %slice_select_fusion), channel_id=1, source_target_pairs={{0,208},{16,64},{32,240},{48,96},{64,16},{80,128},{96,48},{112,160... | collective-permute-start | bytes 24584 | tf_op jit(solution)/shard_map/ppermute | solution.py:18
  8.5 0.7 %copy-start.2 = (s32[16]{0:T(128)S(1)}, s32[16]{0:T(128)}, u32[]{:S(2)}) copy-start(s32[16]{0:T(128)} %param.12) | copy-start | bytes 196
  12.9 6.1 %collective-permute-start.3 = (f32[392,128]{1,0:T(8,128)S(1)}, f32[392,128]{1,0:T(8,128)S(1)}, u32[]{:S(2)}, u32[]{:S(2)}) collective-permute-start(f32[392,128]{1,0:T(8,128)S(1)} %get-tuple-element.9), channel_id=1, source_target_pairs={{0,16},{16,0},{32,48},{48,32},{64,80},{80,64},{96,112},{112,96},{1... | collective-permute-start | bytes 602120 | tf_op jit(solution)/shard_map/ppermute | solution.py:18
  19.9 13.1 %collective-permute-start.4 = (f32[272,128]{1,0:T(8,128)S(1)}, f32[272,128]{1,0:T(8,128)S(1)}, u32[]{:S(2)}, u32[]{:S(2)}) collective-permute-start(f32[272,128]{1,0:T(8,128)S(1)} %get-tuple-element.10.own), channel_id=1, source_target_pairs={{0,2},{2,0},{4,6},{6,4},{8,10},{10,8},{12,14},{14,12},{1,3},{3,1},... | collective-permute-start | bytes 417800 | tf_op jit(solution)/shard_map/ppermute | solution.py:18
  20.0 13.0 %collective-permute-start.5 = (f32[272,128]{1,0:T(8,128)S(1)}, f32[272,128]{1,0:T(8,128)S(1)}, u32[]{:S(2)}, u32[]{:S(2)}) collective-permute-start(f32[272,128]{1,0:T(8,128)S(1)} %get-tuple-element.10.own), channel_id=1, source_target_pairs={{0,14},{2,4},{4,2},{6,8},{8,6},{10,12},{12,10},{14,0},{1,15},{3,5}... | collective-permute-start | bytes 417800 | tf_op jit(solution)/shard_map/ppermute | solution.py:18
  24.6 3.4 %collective-permute-start.8 = (f32[16,128]{1,0:T(8,128)S(1)}, f32[16,128]{1,0:T(8,128)S(1)}, u32[]{:S(2)}, u32[]{:S(2)}) collective-permute-start(f32[16,128]{1,0:T(8,128)S(1)} %get-tuple-element.25), channel_id=1, source_target_pairs={{0,240},{16,32},{32,16},{48,64},{64,48},{80,96},{96,80},{112,128},... | collective-permute-start | bytes 24584 | tf_op jit(solution)/shard_map/ppermute | solution.py:18
  24.6 8.5 %collective-permute-start.6 = (f32[48,128]{1,0:T(8,128)S(1)}, f32[48,128]{1,0:T(8,128)S(1)}, u32[]{:S(2)}, u32[]{:S(2)}) collective-permute-start(f32[48,128]{1,0:T(8,128)S(1)} %get-tuple-element.11), channel_id=1, source_target_pairs={{0,4},{2,6},{4,0},{6,2},{8,12},{10,14},{12,8},{14,10},{1,5},{3,7},... | collective-permute-start | bytes 73736 | tf_op jit(solution)/shard_map/ppermute | solution.py:18
  24.6 8.5 %collective-permute-start.7 = (f32[48,128]{1,0:T(8,128)S(1)}, f32[48,128]{1,0:T(8,128)S(1)}, u32[]{:S(2)}, u32[]{:S(2)}) collective-permute-start(f32[48,128]{1,0:T(8,128)S(1)} %get-tuple-element.11), channel_id=1, source_target_pairs={{0,12},{2,14},{4,8},{6,10},{8,4},{10,6},{12,0},{14,2},{1,13},{3,15... | collective-permute-start | bytes 73736 | tf_op jit(solution)/shard_map/ppermute | solution.py:18
  27.9 5.1 %collective-permute-start.9 = (f32[32,128]{1,0:T(8,128)S(1)}, f32[32,128]{1,0:T(8,128)S(1)}, u32[]{:S(2)}, u32[]{:S(2)}) collective-permute-start(f32[32,128]{1,0:T(8,128)S(1)} %pad_maximum_fusion.mine), channel_id=1, source_target_pairs={{0,16},{16,0},{32,48},{48,32},{64,80},{80,64},{96,112},{112,96},{1... | collective-permute-start | bytes 49160 | tf_op jit(solution)/shard_map/ppermute | solution.py:18
  35.1 3.5 %copy-start.1 = (f32[2,1,128]{2,1,0:T(1,128)S(1)}, f32[2,1,128]{2,1,0:T(1,128)}, u32[]{:S(2)}) copy-start(f32[2,1,128]{2,1,0:T(1,128)} %param.13) | copy-start | bytes 3076
  35.1 10.4 %all-to-all-start = ((f32[8,8,128]{2,1,0:T(8,128)}), f32[8,8,128]{2,1,0:T(8,128)S(1)}, u32[]{:S(2)}, u32[]{:S(2)}) async-start(f32[8,8,128]{2,1,0:T(8,128)} %broadcast_in_dim.16), calls=%async_computation | async-start | bytes 65536 | tf_op jit(solution)/shard_map/all_to_all | solution.py:255
  38.6 14.1 %collective-permute-start.10 = (f32[272,128]{1,0:T(8,128)S(1)}, f32[272,128]{1,0:T(8,128)S(1)}, u32[]{:S(2)}, u32[]{:S(2)}) collective-permute-start(f32[272,128]{1,0:T(8,128)S(1)} %second_shear.1.own.cells), channel_id=1, source_target_pairs={{0,32},{16,48},{32,0},{48,16},{64,96},{80,112},{96,64},{112,80},{1... | collective-permute-start | bytes 417800 | tf_op jit(solution)/shard_map/ppermute | solution.py:18
  38.7 14.0 %collective-permute-start.11 = (f32[272,128]{1,0:T(8,128)S(1)}, f32[272,128]{1,0:T(8,128)S(1)}, u32[]{:S(2)}, u32[]{:S(2)}) collective-permute-start(f32[272,128]{1,0:T(8,128)S(1)} %second_shear.1.own.cells), channel_id=1, source_target_pairs={{0,224},{16,240},{32,64},{48,80},{64,32},{80,48},{96,128},{112,144... | collective-permute-start | bytes 417800 | tf_op jit(solution)/shard_map/ppermute | solution.py:18
  46.2 14.1 %all-to-all-start.1 = ((f32[32,8,128]{2,1,0:T(8,128)}), f32[32,8,128]{2,1,0:T(8,128)S(1)}, u32[]{:S(2)}, u32[]{:S(2)}) async-start(f32[32,8,128]{2,1,0:T(8,128)} %broadcast_in_dim.33), calls=%async_computation.1 | async-start | bytes 262144 | tf_op jit(solution)/shard_map/all_to_all | solution.py:255
  53.5 8.2 %collective-permute-start.12 = (f32[128,128]{1,0:T(8,128)S(1)}, f32[128,128]{1,0:T(8,128)S(1)}, u32[]{:S(2)}, u32[]{:S(2)}) collective-permute-start(f32[128,128]{1,0:T(8,128)S(1)} %get-tuple-element.13), channel_id=1, source_target_pairs={{0,16},{16,0},{32,48},{48,32},{64,80},{80,64},{96,112},{112,96},{1... | collective-permute-start | bytes 196616 | tf_op jit(solution)/shard_map/ppermute | solution.py:18

commit v4 on v3

--- a/solution.py
+++ b/solution.py
@@ -173,13 +173,13 @@
         else:
             out[256:272, :] = summed[0:16, :]
 
-def third_kernel(flags, own, near_a, near_b, params, keep, send, ext):
-    odd, core = flags[0], flags[4]
+def third_kernel(flags, own, below, above, params, keep, send, ext):
+    core = flags[4]
     zero(ext, 0, 8)
-    assemble(ext, 8, 8, odd, near_a, near_b, 264, 264)
-    assemble(ext, 16, 256, odd, near_a, near_b, 0, 0)
+    ext[8:16, :] = below[264:272, :]
+    ext[16:272, :] = below[0:256, :]
     ext[272:528, :] = own[0:256, :]
-    assemble(ext, 528, 264, odd, near_b, near_a, 0, 0)
+    ext[528:792, :] = above[0:264, :]
     zero(ext, 792, 800)
     weights = params[...]
     barrel(ext, 288, 9, SPAN_X - weights[8:9, :].astype(jnp.int32))
@@ -307,7 +307,8 @@
         [(272, B)],
         [(3, 400, B)],
     )
-    near_a, near_b = permuted(second, "gx", ring_x[0]), permuted(second, "gx", ring_x[1])
+    below = permuted(second, "gx", lambda i: (i + 2) % size_x)
+    above = permuted(second, "gx", lambda i: (i - 2) % size_x)
     sums = call(
         depth_sum_kernel,
         "depth_sum",
@@ -323,7 +324,7 @@
         third_kernel,
         "third_shear",
         [flags],
-        [second, near_a, near_b, third_params],
+        [second, below, above, third_params],
         [(B, B), (B, B)],
         [(800, B)],
     )

time: 62.7 us -> 62.7 us (level)
  starting transfers between devices: 35.7 us -> 37.3 us
  waiting for transfers between devices: 14.3 us -> 12.8 us
    ppermute x13, starting transfers between devices: 25.7 us -> 27.3 us  [permuted(): lax.ppermute(value, axis, [(i, target(i)) for i in range(lax.axis_size(ax...]
    all_to_all x2, waiting for transfers between devices: 9.77 us -> 8.2 us  [everywhere(): return lax.all_to_all(copies, axes, 0, 0, tiled=True)]
where the time goes in v4:
time: 62.7 us; the launch traced here: 62.3 us
  starting transfers between devices  37.3 us (59%)
  waiting for transfers between devices  12.8 us (20%)
  Pallas kernels  4.93 us (8%)
  local copies, waits for them, and re-layouts  3.44 us (5%)
  other arithmetic  3.04 us (5%)
  between operations  0.87 us (1%)
    ppermute x13, starting transfers between devices, permuted(): lax.ppermute(value, axis, [(i, target(i)) for i in range(lax.axis_size(ax...  27.3 us
    all_to_all x2, starting transfers between devices, everywhere(): return lax.all_to_all(copies, axes, 0, 0, tiled=True)  9.99 us
    all_to_all x2, waiting for transfers between devices, everywhere(): return lax.all_to_all(copies, axes, 0, 0, tiled=True)  8.2 us
    pallas_call x6, Pallas kernels, call(): pl.pallas_call(kernel, out_shape=[f32(shape) for shape in outs], in_specs...  4.93 us
    ppermute x13, waiting for transfers between devices, permuted(): lax.ppermute(value, axis, [(i, target(i)) for i in range(lax.axis_size(ax...  4.57 us
    broadcast_in_dim x2, local copies, waits for them, and re-layouts, everywhere(): copies = jnp.broadcast_to(value[None], (count,) + value.shape)  1.3 us
  transfers between devices with their start and end apart: 15, of which 6 were waited for; matrix products, arithmetic and copies ran while one was open for 7% of the time, Pallas kernels for 3%

profile of v4, /device:TPU:1, one launch (start us, length us, event | category | flops | bytes accessed | tf_op | source)
XLA Modules:
  0.0 62.3 jit_solution(2450704463529328076)
XLA Ops:
  0.6 2.1 %collective-permute-start = (f32[2,128,128]{2,1,0:T(8,128)}, f32[2,128,128]{2,1,0:T(8,128)S(1)}, u32[]{:S(2)}, u32[]{:S(2)}) collective-permute-start(f32[2,128,128]{2,1,0:T(8,128)} %bitcast.49), channel_id=1, source_target_pairs={{0,32},{16,48},{32,64},{48,80},{64,96},{80,112},{96,128},{112,144}... | collective-permute-start | bytes 393224 | tf_op jit(solution)/shard_map/ppermute | solution.py:18
  2.8 4.0 %collective-permute-start.1 = (f32[2,128,128]{2,1,0:T(8,128)}, f32[2,128,128]{2,1,0:T(8,128)S(1)}, u32[]{:S(2)}, u32[]{:S(2)}) collective-permute-start(f32[2,128,128]{2,1,0:T(8,128)} %bitcast.50), channel_id=1, source_target_pairs={{0,224},{16,240},{32,0},{48,16},{64,32},{80,48},{96,64},{112,80},{... | collective-permute-start | bytes 393224 | tf_op jit(solution)/shard_map/ppermute | solution.py:18
  6.8 0.7 %slice_select_fusion = f32[2,8,128]{2,1,0:T(8,128)S(1)} fusion(f32[2,128,128]{2,1,0:T(8,128)} %bitcast.51, pred[]{:T(512)S(6)} %eq.4), kind=kLoop, calls=%fused_computation.9 | loop fusion | flops 2048 | bytes 24577 | tf_op jit(solution)/shard_map/jit(_where)/select_n | solution.py:275
  7.6 0.9 %select_bitcast_fusion.2 = (f32[128,128]{1,0:T(8,128)S(1)}, f32[128,128]{1,0:T(8,128)S(1)}) fusion(f32[2,1,128,128]{3,2,1,0:T(8,128)} %param.7, pred[]{:T(512)S(6)} %eq.4), kind=kLoop, calls=%fused_computation.3 | loop fusion | flops 32768 | bytes 262145 | tf_op jit(solution)/shard_map/jit(_where)/select_n | solution.py:278
  9.3 0.7 %constant_dynamic-slice_fusion.1 = s32[1,2,128]{2,1,0:T(2,128)S(1)} fusion(s32[16,2,128]{2,1,0:T(2,128)} %param.8, s32[]{:T(128)S(6)} %select_n.72), kind=kLoop, calls=%fused_computation.16 | loop fusion | bytes 2052 | tf_op jit(solution)/shard_map/dynamic_slice | solution.py:287
  10.0 0.7 %dynamic-slice_bitcast_fusion = (f32[8,128]{1,0:T(8,128)S(1)}, f32[8,128]{1,0:T(8,128)S(1)}) fusion(f32[16,2,8,128]{3,2,1,0:T(8,128)} %param.9, s32[]{:T(128)S(6)} %select_n.72, s32[]{:T(128)S(6)} %add.25), kind=kLoop, calls=%fused_computation.10 | loop fusion | bytes 16392 | tf_op jit(solution)/shard_map/squeeze | solution.py:288
  10.8 1.6 %collective-permute-done.2.far = f32[2,8,128]{2,1,0:T(8,128)S(1)} collective-permute-done((f32[2,8,128]{2,1,0:T(8,128)S(1)}, f32[2,8,128]{2,1,0:T(8,128)S(1)}, u32[]{:S(2)}, u32[]{:S(2)}) %collective-permute-start.2) | collective-permute-done | bytes 8224 | tf_op jit(solution)/shard_map/ppermute | solution.py:18
  12.9 5.0 %collective-permute-start.3 = (f32[392,128]{1,0:T(8,128)S(1)}, f32[392,128]{1,0:T(8,128)S(1)}, u32[]{:S(2)}, u32[]{:S(2)}) collective-permute-start(f32[392,128]{1,0:T(8,128)S(1)} %get-tuple-element.9), channel_id=1, source_target_pairs={{0,16},{16,0},{32,48},{48,32},{64,80},{80,64},{96,112},{112,96},{1... | collective-permute-start | bytes 602120 | tf_op jit(solution)/shard_map/ppermute | solution.py:18
  18.0 0.7 %fusion = f32[1,128]{1,0:T(1,128)S(1)} fusion(s32[16,128]{1,0:T(8,128)} %param.10, s32[]{:T(128)S(6)} %select_n.72), kind=kLoop, calls=%fused_computation.17 | loop fusion | flops 128 | bytes 1028 | tf_op jit(solution)/shard_map/convert_element_type | solution.py:267
  19.1 0.8 %first_shear.1 = (f32[272,128]{1,0:T(8,128)S(1)}, f32[48,128]{1,0:T(8,128)S(1)}) custom-call(s32[8]{0:T(128)S(1)} %stack.41.flags, f32[392,128]{1,0:T(8,128)S(1)} %get-tuple-element.8.mine, f32[392,128]{1,0:T(8,128)S(1)} %collective-permute-done.3.got, f32[16,128]{1,0:T(8,128)S(1)} %get-tuple-element.26.params), custom_call_target="tpu_custom_call" | custom-call | tf_op jit(solution)/shard_map/first_shear/pallas_call | solution.py:234
  20.0 4.6 %collective-permute-start.5 = (f32[272,128]{1,0:T(8,128)S(1)}, f32[272,128]{1,0:T(8,128)S(1)}, u32[]{:S(2)}, u32[]{:S(2)}) collective-permute-start(f32[272,128]{1,0:T(8,128)S(1)} %get-tuple-element.10.own), channel_id=1, source_target_pairs={{0,14},{2,4},{4,2},{6,8},{8,6},{10,12},{12,10},{14,0},{1,15},{3,5}... | collective-permute-start | bytes 417800 | tf_op jit(solution)/shard_map/ppermute | solution.py:18
  24.6 1.6 %collective-permute-start.7 = (f32[48,128]{1,0:T(8,128)S(1)}, f32[48,128]{1,0:T(8,128)S(1)}, u32[]{:S(2)}, u32[]{:S(2)}) collective-permute-start(f32[48,128]{1,0:T(8,128)S(1)} %get-tuple-element.11), channel_id=1, source_target_pairs={{0,12},{2,14},{4,8},{6,10},{8,4},{10,6},{12,0},{14,2},{1,13},{3,15... | collective-permute-start | bytes 73736 | tf_op jit(solution)/shard_map/ppermute | solution.py:18
  26.2 1.7 %collective-permute-done.8 = f32[16,128]{1,0:T(8,128)S(1)} collective-permute-done((f32[16,128]{1,0:T(8,128)S(1)}, f32[16,128]{1,0:T(8,128)S(1)}, u32[]{:S(2)}, u32[]{:S(2)}) %collective-permute-start.8) | collective-permute-done | bytes 8224 | tf_op jit(solution)/shard_map/ppermute | solution.py:18
  27.9 4.3 %collective-permute-start.9 = (f32[32,128]{1,0:T(8,128)S(1)}, f32[32,128]{1,0:T(8,128)S(1)}, u32[]{:S(2)}, u32[]{:S(2)}) collective-permute-start(f32[32,128]{1,0:T(8,128)S(1)} %pad_maximum_fusion.mine), channel_id=1, source_target_pairs={{0,16},{16,0},{32,48},{48,32},{64,80},{80,64},{96,112},{112,96},{1... | collective-permute-start | bytes 49160 | tf_op jit(solution)/shard_map/ppermute | solution.py:18
  32.2 0.8 %collective-permute-done.9.got = f32[32,128]{1,0:T(8,128)S(1)} collective-permute-done((f32[32,128]{1,0:T(8,128)S(1)}, f32[32,128]{1,0:T(8,128)S(1)}, u32[]{:S(2)}, u32[]{:S(2)}) %collective-permute-start.9) | collective-permute-done | bytes 16416 | tf_op jit(solution)/shard_map/ppermute | solution.py:18
  33.1 0.9 %second_shear.1.own.cells = f32[272,128]{1,0:T(8,128)S(1)} custom-call(s32[8]{0:T(128)S(1)} %stack.41.flags, f32[272,128]{1,0:T(8,128)S(1)} %get-tuple-element.10.own, f32[272,128]{1,0:T(8,128)S(1)} %collective-permute-done.4.near_a, f32[272,128]{1,0:T(8,128)S(1)} %collective-permute-done.5.near_b, f32[48,128]{1,0:T(8,128)S(1)} %collective-permute-done.6.far_a, ...), custom_call_target="tpu_custom_call" | custom-call | tf_op jit(solution)/shard_map/second_shear/pallas_call | solution.py:234
  35.1 3.5 %all-to-all-start = ((f32[8,8,128]{2,1,0:T(8,128)}), f32[8,8,128]{2,1,0:T(8,128)S(1)}, u32[]{:S(2)}, u32[]{:S(2)}) async-start(f32[8,8,128]{2,1,0:T(8,128)} %broadcast_in_dim.16), calls=%async_computation | async-start | bytes 65536 | tf_op jit(solution)/shard_map/all_to_all | solution.py:255
  38.7 5.1 %collective-permute-start.11 = (f32[272,128]{1,0:T(8,128)S(1)}, f32[272,128]{1,0:T(8,128)S(1)}, u32[]{:S(2)}, u32[]{:S(2)}) collective-permute-start(f32[272,128]{1,0:T(8,128)S(1)} %second_shear.1.own.cells), channel_id=1, source_target_pairs={{0,224},{16,240},{32,0},{48,16},{64,32},{80,48},{96,64},{112,80},{... | collective-permute-start | bytes 417800 | tf_op jit(solution)/shard_map/ppermute | solution.py:18
  43.8 1.7 %all-to-all-done = f32[8,8,128]{2,1,0:T(8,128)S(1)} async-done(((f32[8,8,128]{2,1,0:T(8,128)}), f32[8,8,128]{2,1,0:T(8,128)S(1)}, u32[]{:S(2)}, u32[]{:S(2)}) %all-to-all-start) | async-done | bytes 32800 | tf_op jit(solution)/shard_map/all_to_all | solution.py:255
  45.5 0.7 %broadcast_in_dim.33 = f32[32,8,128]{2,1,0:T(8,128)} broadcast(f32[8,128]{1,0:T(8,128)S(1)} %pad_maximum_fusion.4), dimensions={1,2} | broadcast | bytes 135168 | tf_op jit(solution)/shard_map/broadcast_in_dim | solution.py:254
  46.2 6.5 %all-to-all-start.1 = ((f32[32,8,128]{2,1,0:T(8,128)}), f32[32,8,128]{2,1,0:T(8,128)S(1)}, u32[]{:S(2)}, u32[]{:S(2)}) async-start(f32[32,8,128]{2,1,0:T(8,128)} %broadcast_in_dim.33), calls=%async_computation.1 | async-start | bytes 262144 | tf_op jit(solution)/shard_map/all_to_all | solution.py:255
  52.7 0.7 %third_shear.1 = (f32[128,128]{1,0:T(8,128)S(1)}, f32[128,128]{1,0:T(8,128)S(1)}) custom-call(s32[8]{0:T(128)S(1)} %stack.41.flags, f32[272,128]{1,0:T(8,128)S(1)} %second_shear.1.own.cells, f32[272,128]{1,0:T(8,128)S(1)} %collective-permute-done.10.below, f32[272,128]{1,0:T(8,128)S(1)} %collective-permute-done.11.above, f32[16,128]{1,0:T(8,128)S(1)} %get-tuple-element.24.params), custom_call_target="tpu_custom_call" | custom-call | tf_op jit(solution)/shard_map/third_shear/pallas_call | solution.py:234
  53.8 6.5 %all-to-all-done.1.gathered = f32[32,8,128]{2,1,0:T(8,128)S(1)} async-done(((f32[32,8,128]{2,1,0:T(8,128)}), f32[32,8,128]{2,1,0:T(8,128)S(1)}, u32[]{:S(2)}, u32[]{:S(2)}) %all-to-all-start.1) | async-done | bytes 131104 | tf_op jit(solution)/shard_map/all_to_all | solution.py:255
  60.3 1.4 %exit_wave.1 = f32[2,128]{1,0:T(2,128)} custom-call(s32[8]{0:T(128)S(1)} %stack.41.flags, f32[32,8,128]{2,1,0:T(8,128)S(1)} %all-to-all-done.1.gathered, f32[2,128]{1,0:T(2,128)S(1)} %bitcast.48), custom_call_target="tpu_custom_call" | custom-call | tf_op jit(solution)/shard_map/exit_wave/pallas_call | solution.py:234
  (36 shorter events, 4.2 us)
Async XLA Ops:
  0.6 10.0 %copy-start = (f32[16,8,128]{2,1,0:T(8,128)S(1)}, f32[16,8,128]{2,1,0:T(8,128)}, u32[]{:S(2)}) copy-start(f32[16,8,128]{2,1,0:T(8,128)} %param.11) | copy-start | bytes 196612
  0.6 11.7 %collective-permute-start = (f32[2,128,128]{2,1,0:T(8,128)}, f32[2,128,128]{2,1,0:T(8,128)S(1)}, u32[]{:S(2)}, u32[]{:S(2)}) collective-permute-start(f32[2,128,128]{2,1,0:T(8,128)} %bitcast.49), channel_id=1, source_target_pairs={{0,32},{16,48},{32,64},{48,80},{64,96},{80,112},{96,128},{112,144}... | collective-permute-start | bytes 393224 | tf_op jit(solution)/shard_map/ppermute | solution.py:18
  2.8 9.6 %collective-permute-start.1 = (f32[2,128,128]{2,1,0:T(8,128)}, f32[2,128,128]{2,1,0:T(8,128)S(1)}, u32[]{:S(2)}, u32[]{:S(2)}) collective-permute-start(f32[2,128,128]{2,1,0:T(8,128)} %bitcast.50), channel_id=1, source_target_pairs={{0,224},{16,240},{32,0},{48,16},{64,32},{80,48},{96,64},{112,80},{... | collective-permute-start | bytes 393224 | tf_op jit(solution)/shard_map/ppermute | solution.py:18
  7.5 4.9 %collective-permute-start.2 = (f32[2,8,128]{2,1,0:T(8,128)S(1)}, f32[2,8,128]{2,1,0:T(8,128)S(1)}, u32[]{:S(2)}, u32[]{:S(2)}) collective-permute-start(f32[2,8,128]{2,1,0:T(8,128)S(1)} %slice_select_fusion), channel_id=1, source_target_pairs={{0,208},{16,64},{32,240},{48,96},{64,16},{80,128},{96,48},{112,160... | collective-permute-start | bytes 24584 | tf_op jit(solution)/shard_map/ppermute | solution.py:18
  8.5 0.7 %copy-start.2 = (s32[16]{0:T(128)S(1)}, s32[16]{0:T(128)}, u32[]{:S(2)}) copy-start(s32[16]{0:T(128)} %param.12) | copy-start | bytes 196
  12.9 6.1 %collective-permute-start.3 = (f32[392,128]{1,0:T(8,128)S(1)}, f32[392,128]{1,0:T(8,128)S(1)}, u32[]{:S(2)}, u32[]{:S(2)}) collective-permute-start(f32[392,128]{1,0:T(8,128)S(1)} %get-tuple-element.9), channel_id=1, source_target_pairs={{0,16},{16,0},{32,48},{48,32},{64,80},{80,64},{96,112},{112,96},{1... | collective-permute-start | bytes 602120 | tf_op jit(solution)/shard_map/ppermute | solution.py:18
  19.9 13.1 %collective-permute-start.4 = (f32[272,128]{1,0:T(8,128)S(1)}, f32[272,128]{1,0:T(8,128)S(1)}, u32[]{:S(2)}, u32[]{:S(2)}) collective-permute-start(f32[272,128]{1,0:T(8,128)S(1)} %get-tuple-element.10.own), channel_id=1, source_target_pairs={{0,2},{2,0},{4,6},{6,4},{8,10},{10,8},{12,14},{14,12},{1,3},{3,1},... | collective-permute-start | bytes 417800 | tf_op jit(solution)/shard_map/ppermute | solution.py:18
  20.0 13.0 %collective-permute-start.5 = (f32[272,128]{1,0:T(8,128)S(1)}, f32[272,128]{1,0:T(8,128)S(1)}, u32[]{:S(2)}, u32[]{:S(2)}) collective-permute-start(f32[272,128]{1,0:T(8,128)S(1)} %get-tuple-element.10.own), channel_id=1, source_target_pairs={{0,14},{2,4},{4,2},{6,8},{8,6},{10,12},{12,10},{14,0},{1,15},{3,5}... | collective-permute-start | bytes 417800 | tf_op jit(solution)/shard_map/ppermute | solution.py:18
  24.6 3.4 %collective-permute-start.8 = (f32[16,128]{1,0:T(8,128)S(1)}, f32[16,128]{1,0:T(8,128)S(1)}, u32[]{:S(2)}, u32[]{:S(2)}) collective-permute-start(f32[16,128]{1,0:T(8,128)S(1)} %get-tuple-element.25), channel_id=1, source_target_pairs={{0,240},{16,32},{32,16},{48,64},{64,48},{80,96},{96,80},{112,128},... | collective-permute-start | bytes 24584 | tf_op jit(solution)/shard_map/ppermute | solution.py:18
  24.6 8.5 %collective-permute-start.6 = (f32[48,128]{1,0:T(8,128)S(1)}, f32[48,128]{1,0:T(8,128)S(1)}, u32[]{:S(2)}, u32[]{:S(2)}) collective-permute-start(f32[48,128]{1,0:T(8,128)S(1)} %get-tuple-element.11), channel_id=1, source_target_pairs={{0,4},{2,6},{4,0},{6,2},{8,12},{10,14},{12,8},{14,10},{1,5},{3,7},... | collective-permute-start | bytes 73736 | tf_op jit(solution)/shard_map/ppermute | solution.py:18
  24.6 8.5 %collective-permute-start.7 = (f32[48,128]{1,0:T(8,128)S(1)}, f32[48,128]{1,0:T(8,128)S(1)}, u32[]{:S(2)}, u32[]{:S(2)}) collective-permute-start(f32[48,128]{1,0:T(8,128)S(1)} %get-tuple-element.11), channel_id=1, source_target_pairs={{0,12},{2,14},{4,8},{6,10},{8,4},{10,6},{12,0},{14,2},{1,13},{3,15... | collective-permute-start | bytes 73736 | tf_op jit(solution)/shard_map/ppermute | solution.py:18
  27.9 5.1 %collective-permute-start.9 = (f32[32,128]{1,0:T(8,128)S(1)}, f32[32,128]{1,0:T(8,128)S(1)}, u32[]{:S(2)}, u32[]{:S(2)}) collective-permute-start(f32[32,128]{1,0:T(8,128)S(1)} %pad_maximum_fusion.mine), channel_id=1, source_target_pairs={{0,16},{16,0},{32,48},{48,32},{64,80},{80,64},{96,112},{112,96},{1... | collective-permute-start | bytes 49160 | tf_op jit(solution)/shard_map/ppermute | solution.py:18
  35.1 3.5 %copy-start.1 = (f32[2,1,128]{2,1,0:T(1,128)S(1)}, f32[2,1,128]{2,1,0:T(1,128)}, u32[]{:S(2)}) copy-start(f32[2,1,128]{2,1,0:T(1,128)} %param.13) | copy-start | bytes 3076
  35.1 10.4 %all-to-all-start = ((f32[8,8,128]{2,1,0:T(8,128)}), f32[8,8,128]{2,1,0:T(8,128)S(1)}, u32[]{:S(2)}, u32[]{:S(2)}) async-start(f32[8,8,128]{2,1,0:T(8,128)} %broadcast_in_dim.16), calls=%async_computation | async-start | bytes 65536 | tf_op jit(solution)/shard_map/all_to_all | solution.py:255
  38.6 14.1 %collective-permute-start.10 = (f32[272,128]{1,0:T(8,128)S(1)}, f32[272,128]{1,0:T(8,128)S(1)}, u32[]{:S(2)}, u32[]{:S(2)}) collective-permute-start(f32[272,128]{1,0:T(8,128)S(1)} %second_shear.1.own.cells), channel_id=1, source_target_pairs={{0,32},{16,48},{32,64},{48,80},{64,96},{80,112},{96,128},{112,144}... | collective-permute-start | bytes 417800 | tf_op jit(solution)/shard_map/ppermute | solution.py:18
  38.7 14.0 %collective-permute-start.11 = (f32[272,128]{1,0:T(8,128)S(1)}, f32[272,128]{1,0:T(8,128)S(1)}, u32[]{:S(2)}, u32[]{:S(2)}) collective-permute-start(f32[272,128]{1,0:T(8,128)S(1)} %second_shear.1.own.cells), channel_id=1, source_target_pairs={{0,224},{16,240},{32,0},{48,16},{64,32},{80,48},{96,64},{112,80},{... | collective-permute-start | bytes 417800 | tf_op jit(solution)/shard_map/ppermute | solution.py:18
  46.2 14.1 %all-to-all-start.1 = ((f32[32,8,128]{2,1,0:T(8,128)}), f32[32,8,128]{2,1,0:T(8,128)S(1)}, u32[]{:S(2)}, u32[]{:S(2)}) async-start(f32[32,8,128]{2,1,0:T(8,128)} %broadcast_in_dim.33), calls=%async_computation.1 | async-start | bytes 262144 | tf_op jit(solution)/shard_map/all_to_all | solution.py:255
  53.5 8.2 %collective-permute-start.12 = (f32[128,128]{1,0:T(8,128)S(1)}, f32[128,128]{1,0:T(8,128)S(1)}, u32[]{:S(2)}, u32[]{:S(2)}) collective-permute-start(f32[128,128]{1,0:T(8,128)S(1)} %get-tuple-element.13), channel_id=1, source_target_pairs={{0,16},{16,0},{32,48},{48,32},{64,80},{80,64},{96,112},{112,96},{1... | collective-permute-start | bytes 196616 | tf_op jit(solution)/shard_map/ppermute | solution.py:18

commit v5 on v3

--- a/solution.py
+++ b/solution.py
@@ -98,23 +98,23 @@
     out[...] = padded[0:8, :]
 
 
-def pack_kernel(
-    flags, mine_own, theirs_own, below, above, far, mine, theirs
-):
+def pack_kernel(flags, own, below, above, far, out):
+    channel = 1 - flags[4]
+    out[0:128, :] = own[...]
+    out[128:256, :] = below[channel]
+    out[256:384, :] = above[channel]
+    out[384:392, :] = far[channel]
+
+
+def first_kernel(flags, own, below, above, far, got, params, out, edges, ext, rows):
     core = flags[4]
-    for out, channel, own in ((mine, core, mine_own), (theirs, 1 - core, theirs_own)):
-        out[0:128, :] = own[...]
-        out[128:256, :] = below[channel]
-        out[256:384, :] = above[channel]
-        out[384:392, :] = far[channel]
-
-
-def first_kernel(flags, mine, got, params, out, edges, ext, rows):
-    core = flags[4]
 
     def of_core(number, start, size):
-        here, there = mine[pl.ds(start, size), :], got[pl.ds(start, size), :]
-        return jnp.where(core == number, here, there)
+        if start == 0:
+            here = own[...]
+        else:
+            here = {128: below, 256: above, 384: far}[start][core]
+        return jnp.where(core == number, here, got[pl.ds(start, size), :])
 
     zero(ext, 0, 8)
     ext[8:16, :] = of_core(0, 384, 8)
@@ -276,13 +276,9 @@
     beside = permuted(columns, "gx", outward(1))
     swap = lambda i: i ^ 1
     pair = lambda a, b: [jnp.where(core == 0, a, b), jnp.where(core == 0, b, a)]
-    mine, theirs = call(
-        pack_kernel,
-        "pack",
-        [flags],
-        [*pair(slab[0], slab[1]), below, above, far],
-        [(392, B), (392, B)],
-        [],
+    mine, theirs = pair(slab[0], slab[1])
+    theirs = call(
+        pack_kernel, "pack", [flags], [theirs, below, above, far], [(392, B)], []
     )
     hops, taps = depth_hops[which], depth_taps[which]
     first_params, third_params = params(taps[0], hops[0]), params(taps[1], hops[1])
@@ -291,7 +287,7 @@
         first_kernel,
         "first_shear",
         [flags],
-        [mine, got, first_params],
+        [mine, below, above, far, got, first_params],
         [(272, B), (48, B)],
         [(800, B), (256, B)],
     )

time: 62.7 us -> 62.7 us (level)
  no operation moved by 1% of the time
where the time goes in v5:
time: 62.7 us; the launch traced here: 62.3 us
  starting transfers between devices  35.8 us (57%)
  waiting for transfers between devices  14.2 us (23%)
  Pallas kernels  4.93 us (8%)
  local copies, waits for them, and re-layouts  3.44 us (5%)
  other arithmetic  3.04 us (5%)
  between operations  0.87 us (1%)
    ppermute x13, starting transfers between devices, permuted(): lax.ppermute(value, axis, [(i, target(i)) for i in range(lax.axis_size(ax...  25.7 us
    all_to_all x2, starting transfers between devices, everywhere(): return lax.all_to_all(copies, axes, 0, 0, tiled=True)  10.1 us
    all_to_all x2, waiting for transfers between devices, everywhere(): return lax.all_to_all(copies, axes, 0, 0, tiled=True)  9.67 us
    pallas_call x6, Pallas kernels, call(): pl.pallas_call(kernel, out_shape=[f32(shape) for shape in outs], in_specs...  4.93 us
    ppermute x13, waiting for transfers between devices, permuted(): lax.ppermute(value, axis, [(i, target(i)) for i in range(lax.axis_size(ax...  4.57 us
    broadcast_in_dim x2, local copies, waits for them, and re-layouts, everywhere(): copies = jnp.broadcast_to(value[None], (count,) + value.shape)  1.3 us
  transfers between devices with their start and end apart: 15, of which 6 were waited for; matrix products, arithmetic and copies ran while one was open for 7% of the time, Pallas kernels for 3%

profile of v5, /device:TPU:1, one launch (start us, length us, event | category | flops | bytes accessed | tf_op | source)
XLA Modules:
  0.0 62.3 jit_solution(12703745492751488669)
XLA Ops:
  0.6 2.1 %collective-permute-start = (f32[2,128,128]{2,1,0:T(8,128)}, f32[2,128,128]{2,1,0:T(8,128)S(1)}, u32[]{:S(2)}, u32[]{:S(2)}) collective-permute-start(f32[2,128,128]{2,1,0:T(8,128)} %bitcast.49), channel_id=1, source_target_pairs={{0,32},{16,48},{32,64},{48,80},{64,96},{80,112},{96,128},{112,144}... | collective-permute-start | bytes 393224 | tf_op jit(solution)/shard_map/ppermute | solution.py:18
  2.8 4.0 %collective-permute-start.1 = (f32[2,128,128]{2,1,0:T(8,128)}, f32[2,128,128]{2,1,0:T(8,128)S(1)}, u32[]{:S(2)}, u32[]{:S(2)}) collective-permute-start(f32[2,128,128]{2,1,0:T(8,128)} %bitcast.50), channel_id=1, source_target_pairs={{0,224},{16,240},{32,0},{48,16},{64,32},{80,48},{96,64},{112,80},{... | collective-permute-start | bytes 393224 | tf_op jit(solution)/shard_map/ppermute | solution.py:18
  6.8 0.7 %slice_select_fusion = f32[2,8,128]{2,1,0:T(8,128)S(1)} fusion(f32[2,128,128]{2,1,0:T(8,128)} %bitcast.51, pred[]{:T(512)S(6)} %eq.4), kind=kLoop, calls=%fused_computation.9 | loop fusion | flops 2048 | bytes 24577 | tf_op jit(solution)/shard_map/jit(_where)/select_n | solution.py:275
  7.6 0.9 %select_bitcast_fusion.2 = (f32[128,128]{1,0:T(8,128)S(1)}, f32[128,128]{1,0:T(8,128)S(1)}) fusion(f32[2,1,128,128]{3,2,1,0:T(8,128)} %param.7, pred[]{:T(512)S(6)} %eq.4), kind=kLoop, calls=%fused_computation.3 | loop fusion | flops 32768 | bytes 262145 | tf_op jit(solution)/shard_map/jit(_where)/select_n | solution.py:278
  9.3 0.7 %constant_dynamic-slice_fusion.1 = s32[1,2,128]{2,1,0:T(2,128)S(1)} fusion(s32[16,2,128]{2,1,0:T(2,128)} %param.8, s32[]{:T(128)S(6)} %select_n.72), kind=kLoop, calls=%fused_computation.16 | loop fusion | bytes 2052 | tf_op jit(solution)/shard_map/dynamic_slice | solution.py:283
  10.0 0.7 %dynamic-slice_bitcast_fusion = (f32[8,128]{1,0:T(8,128)S(1)}, f32[8,128]{1,0:T(8,128)S(1)}) fusion(f32[16,2,8,128]{3,2,1,0:T(8,128)} %param.9, s32[]{:T(128)S(6)} %select_n.72, s32[]{:T(128)S(6)} %add.25), kind=kLoop, calls=%fused_computation.10 | loop fusion | bytes 16392 | tf_op jit(solution)/shard_map/squeeze | solution.py:284
  10.8 1.6 %collective-permute-done.2.far = f32[2,8,128]{2,1,0:T(8,128)S(1)} collective-permute-done((f32[2,8,128]{2,1,0:T(8,128)S(1)}, f32[2,8,128]{2,1,0:T(8,128)S(1)}, u32[]{:S(2)}, u32[]{:S(2)}) %collective-permute-start.2) | collective-permute-done | bytes 8224 | tf_op jit(solution)/shard_map/ppermute | solution.py:18
  12.9 5.0 %collective-permute-start.3 = (f32[392,128]{1,0:T(8,128)S(1)}, f32[392,128]{1,0:T(8,128)S(1)}, u32[]{:S(2)}, u32[]{:S(2)}) collective-permute-start(f32[392,128]{1,0:T(8,128)S(1)} %pack.1), channel_id=1, source_target_pairs={{0,16},{16,0},{32,48},{48,32},{64,80},{80,64},{96,112},{112,96},{1... | collective-permute-start | bytes 602120 | tf_op jit(solution)/shard_map/ppermute | solution.py:18
  18.0 0.7 %fusion = f32[1,128]{1,0:T(1,128)S(1)} fusion(s32[16,128]{1,0:T(8,128)} %param.10, s32[]{:T(128)S(6)} %select_n.72), kind=kLoop, calls=%fused_computation.17 | loop fusion | flops 128 | bytes 1028 | tf_op jit(solution)/shard_map/convert_element_type | solution.py:267
  19.1 0.8 %first_shear.1 = (f32[272,128]{1,0:T(8,128)S(1)}, f32[48,128]{1,0:T(8,128)S(1)}) custom-call(s32[8]{0:T(128)S(1)} %stack.41.flags, f32[128,128]{1,0:T(8,128)S(1)} %get-tuple-element.19.own, f32[2,128,128]{2,1,0:T(8,128)S(1)} %collective-permute-done.below, f32[2,128,128]{2,1,0:T(8,128)S(1)} %collective-permute-done.1.above, ...), custom_call_target="tpu_custom_call" | custom-call | tf_op jit(solution)/shard_map/first_shear/pallas_call | solution.py:234
  20.0 4.6 %collective-permute-start.5 = (f32[272,128]{1,0:T(8,128)S(1)}, f32[272,128]{1,0:T(8,128)S(1)}, u32[]{:S(2)}, u32[]{:S(2)}) collective-permute-start(f32[272,128]{1,0:T(8,128)S(1)} %get-tuple-element.6.own), channel_id=1, source_target_pairs={{0,14},{2,4},{4,2},{6,8},{8,6},{10,12},{12,10},{14,0},{1,15},{3,5}... | collective-permute-start | bytes 417800 | tf_op jit(solution)/shard_map/ppermute | solution.py:18
  24.6 1.6 %collective-permute-start.7 = (f32[48,128]{1,0:T(8,128)S(1)}, f32[48,128]{1,0:T(8,128)S(1)}, u32[]{:S(2)}, u32[]{:S(2)}) collective-permute-start(f32[48,128]{1,0:T(8,128)S(1)} %get-tuple-element.7), channel_id=1, source_target_pairs={{0,12},{2,14},{4,8},{6,10},{8,4},{10,6},{12,0},{14,2},{1,13},{3,15... | collective-permute-start | bytes 73736 | tf_op jit(solution)/shard_map/ppermute | solution.py:18
  26.2 1.7 %collective-permute-done.8 = f32[16,128]{1,0:T(8,128)S(1)} collective-permute-done((f32[16,128]{1,0:T(8,128)S(1)}, f32[16,128]{1,0:T(8,128)S(1)}, u32[]{:S(2)}, u32[]{:S(2)}) %collective-permute-start.8) | collective-permute-done | bytes 8224 | tf_op jit(solution)/shard_map/ppermute | solution.py:18
  27.9 4.3 %collective-permute-start.9 = (f32[32,128]{1,0:T(8,128)S(1)}, f32[32,128]{1,0:T(8,128)S(1)}, u32[]{:S(2)}, u32[]{:S(2)}) collective-permute-start(f32[32,128]{1,0:T(8,128)S(1)} %pad_maximum_fusion.mine), channel_id=1, source_target_pairs={{0,16},{16,0},{32,48},{48,32},{64,80},{80,64},{96,112},{112,96},{1... | collective-permute-start | bytes 49160 | tf_op jit(solution)/shard_map/ppermute | solution.py:18
  32.2 0.8 %collective-permute-done.9.got = f32[32,128]{1,0:T(8,128)S(1)} collective-permute-done((f32[32,128]{1,0:T(8,128)S(1)}, f32[32,128]{1,0:T(8,128)S(1)}, u32[]{:S(2)}, u32[]{:S(2)}) %collective-permute-start.9) | collective-permute-done | bytes 16416 | tf_op jit(solution)/shard_map/ppermute | solution.py:18
  33.0 0.9 %second_shear.1.own.cells = f32[272,128]{1,0:T(8,128)S(1)} custom-call(s32[8]{0:T(128)S(1)} %stack.41.flags, f32[272,128]{1,0:T(8,128)S(1)} %get-tuple-element.6.own, f32[272,128]{1,0:T(8,128)S(1)} %collective-permute-done.4.near_a, f32[272,128]{1,0:T(8,128)S(1)} %collective-permute-done.5.near_b, f32[48,128]{1,0:T(8,128)S(1)} %collective-permute-done.6.far_a, ...), custom_call_target="tpu_custom_call" | custom-call | tf_op jit(solution)/shard_map/second_shear/pallas_call | solution.py:234
  35.1 3.5 %all-to-all-start = ((f32[8,8,128]{2,1,0:T(8,128)}), f32[8,8,128]{2,1,0:T(8,128)S(1)}, u32[]{:S(2)}, u32[]{:S(2)}) async-start(f32[8,8,128]{2,1,0:T(8,128)} %broadcast_in_dim.16), calls=%async_computation | async-start | bytes 65536 | tf_op jit(solution)/shard_map/all_to_all | solution.py:255
  38.7 3.5 %collective-permute-start.11 = (f32[272,128]{1,0:T(8,128)S(1)}, f32[272,128]{1,0:T(8,128)S(1)}, u32[]{:S(2)}, u32[]{:S(2)}) collective-permute-start(f32[272,128]{1,0:T(8,128)S(1)} %second_shear.1.own.cells), channel_id=1, source_target_pairs={{0,224},{16,240},{32,64},{48,80},{64,32},{80,48},{96,128},{112,144... | collective-permute-start | bytes 417800 | tf_op jit(solution)/shard_map/ppermute | solution.py:18
  42.2 3.2 %all-to-all-done = f32[8,8,128]{2,1,0:T(8,128)S(1)} async-done(((f32[8,8,128]{2,1,0:T(8,128)}), f32[8,8,128]{2,1,0:T(8,128)S(1)}, u32[]{:S(2)}, u32[]{:S(2)}) %all-to-all-start) | async-done | bytes 32800 | tf_op jit(solution)/shard_map/all_to_all | solution.py:255
  45.4 0.7 %broadcast_in_dim.33 = f32[32,8,128]{2,1,0:T(8,128)} broadcast(f32[8,128]{1,0:T(8,128)S(1)} %pad_maximum_fusion.4), dimensions={1,2} | broadcast | bytes 135168 | tf_op jit(solution)/shard_map/broadcast_in_dim | solution.py:254
  46.1 6.6 %all-to-all-start.1 = ((f32[32,8,128]{2,1,0:T(8,128)}), f32[32,8,128]{2,1,0:T(8,128)S(1)}, u32[]{:S(2)}, u32[]{:S(2)}) async-start(f32[32,8,128]{2,1,0:T(8,128)} %broadcast_in_dim.33), calls=%async_computation.1 | async-start | bytes 262144 | tf_op jit(solution)/shard_map/all_to_all | solution.py:255
  52.7 0.8 %third_shear.1 = (f32[128,128]{1,0:T(8,128)S(1)}, f32[128,128]{1,0:T(8,128)S(1)}) custom-call(s32[8]{0:T(128)S(1)} %stack.41.flags, f32[272,128]{1,0:T(8,128)S(1)} %second_shear.1.own.cells, f32[272,128]{1,0:T(8,128)S(1)} %collective-permute-done.10.near_a, f32[272,128]{1,0:T(8,128)S(1)} %collective-permute-done.11.near_b, ...), custom_call_target="tpu_custom_call" | custom-call | tf_op jit(solution)/shard_map/third_shear/pallas_call | solution.py:234
  53.8 6.5 %all-to-all-done.1.gathered = f32[32,8,128]{2,1,0:T(8,128)S(1)} async-done(((f32[32,8,128]{2,1,0:T(8,128)}), f32[32,8,128]{2,1,0:T(8,128)S(1)}, u32[]{:S(2)}, u32[]{:S(2)}) %all-to-all-start.1) | async-done | bytes 131104 | tf_op jit(solution)/shard_map/all_to_all | solution.py:255
  60.3 1.4 %exit_wave.1 = f32[2,128]{1,0:T(2,128)} custom-call(s32[8]{0:T(128)S(1)} %stack.41.flags, f32[32,8,128]{2,1,0:T(8,128)S(1)} %all-to-all-done.1.gathered, f32[2,128]{1,0:T(2,128)S(1)} %bitcast.48), custom_call_target="tpu_custom_call" | custom-call | tf_op jit(solution)/shard_map/exit_wave/pallas_call | solution.py:234
  (36 shorter events, 4.2 us)
Async XLA Ops:
  0.6 10.0 %copy-start = (f32[16,8,128]{2,1,0:T(8,128)S(1)}, f32[16,8,128]{2,1,0:T(8,128)}, u32[]{:S(2)}) copy-start(f32[16,8,128]{2,1,0:T(8,128)} %param.11) | copy-start | bytes 196612
  0.6 11.7 %collective-permute-start = (f32[2,128,128]{2,1,0:T(8,128)}, f32[2,128,128]{2,1,0:T(8,128)S(1)}, u32[]{:S(2)}, u32[]{:S(2)}) collective-permute-start(f32[2,128,128]{2,1,0:T(8,128)} %bitcast.49), channel_id=1, source_target_pairs={{0,32},{16,48},{32,64},{48,80},{64,96},{80,112},{96,128},{112,144}... | collective-permute-start | bytes 393224 | tf_op jit(solution)/shard_map/ppermute | solution.py:18
  2.8 9.6 %collective-permute-start.1 = (f32[2,128,128]{2,1,0:T(8,128)}, f32[2,128,128]{2,1,0:T(8,128)S(1)}, u32[]{:S(2)}, u32[]{:S(2)}) collective-permute-start(f32[2,128,128]{2,1,0:T(8,128)} %bitcast.50), channel_id=1, source_target_pairs={{0,224},{16,240},{32,0},{48,16},{64,32},{80,48},{96,64},{112,80},{... | collective-permute-start | bytes 393224 | tf_op jit(solution)/shard_map/ppermute | solution.py:18
  7.5 4.9 %collective-permute-start.2 = (f32[2,8,128]{2,1,0:T(8,128)S(1)}, f32[2,8,128]{2,1,0:T(8,128)S(1)}, u32[]{:S(2)}, u32[]{:S(2)}) collective-permute-start(f32[2,8,128]{2,1,0:T(8,128)S(1)} %slice_select_fusion), channel_id=1, source_target_pairs={{0,208},{16,64},{32,240},{48,96},{64,16},{80,128},{96,48},{112,160... | collective-permute-start | bytes 24584 | tf_op jit(solution)/shard_map/ppermute | solution.py:18
  8.5 0.7 %copy-start.2 = (s32[16]{0:T(128)S(1)}, s32[16]{0:T(128)}, u32[]{:S(2)}) copy-start(s32[16]{0:T(128)} %param.12) | copy-start | bytes 196
  12.9 6.1 %collective-permute-start.3 = (f32[392,128]{1,0:T(8,128)S(1)}, f32[392,128]{1,0:T(8,128)S(1)}, u32[]{:S(2)}, u32[]{:S(2)}) collective-permute-start(f32[392,128]{1,0:T(8,128)S(1)} %pack.1), channel_id=1, source_target_pairs={{0,16},{16,0},{32,48},{48,32},{64,80},{80,64},{96,112},{112,96},{1... | collective-permute-start | bytes 602120 | tf_op jit(solution)/shard_map/ppermute | solution.py:18
  19.9 13.1 %collective-permute-start.4 = (f32[272,128]{1,0:T(8,128)S(1)}, f32[272,128]{1,0:T(8,128)S(1)}, u32[]{:S(2)}, u32[]{:S(2)}) collective-permute-start(f32[272,128]{1,0:T(8,128)S(1)} %get-tuple-element.6.own), channel_id=1, source_target_pairs={{0,2},{2,0},{4,6},{6,4},{8,10},{10,8},{12,14},{14,12},{1,3},{3,1},... | collective-permute-start | bytes 417800 | tf_op jit(solution)/shard_map/ppermute | solution.py:18
  20.0 13.0 %collective-permute-start.5 = (f32[272,128]{1,0:T(8,128)S(1)}, f32[272,128]{1,0:T(8,128)S(1)}, u32[]{:S(2)}, u32[]{:S(2)}) collective-permute-start(f32[272,128]{1,0:T(8,128)S(1)} %get-tuple-element.6.own), channel_id=1, source_target_pairs={{0,14},{2,4},{4,2},{6,8},{8,6},{10,12},{12,10},{14,0},{1,15},{3,5}... | collective-permute-start | bytes 417800 | tf_op jit(solution)/shard_map/ppermute | solution.py:18
  24.5 3.4 %collective-permute-start.8 = (f32[16,128]{1,0:T(8,128)S(1)}, f32[16,128]{1,0:T(8,128)S(1)}, u32[]{:S(2)}, u32[]{:S(2)}) collective-permute-start(f32[16,128]{1,0:T(8,128)S(1)} %get-tuple-element.21), channel_id=1, source_target_pairs={{0,240},{16,32},{32,16},{48,64},{64,48},{80,96},{96,80},{112,128},... | collective-permute-start | bytes 24584 | tf_op jit(solution)/shard_map/ppermute | solution.py:18
  24.6 8.5 %collective-permute-start.6 = (f32[48,128]{1,0:T(8,128)S(1)}, f32[48,128]{1,0:T(8,128)S(1)}, u32[]{:S(2)}, u32[]{:S(2)}) collective-permute-start(f32[48,128]{1,0:T(8,128)S(1)} %get-tuple-element.7), channel_id=1, source_target_pairs={{0,4},{2,6},{4,0},{6,2},{8,12},{10,14},{12,8},{14,10},{1,5},{3,7},... | collective-permute-start | bytes 73736 | tf_op jit(solution)/shard_map/ppermute | solution.py:18
  24.6 8.5 %collective-permute-start.7 = (f32[48,128]{1,0:T(8,128)S(1)}, f32[48,128]{1,0:T(8,128)S(1)}, u32[]{:S(2)}, u32[]{:S(2)}) collective-permute-start(f32[48,128]{1,0:T(8,128)S(1)} %get-tuple-element.7), channel_id=1, source_target_pairs={{0,12},{2,14},{4,8},{6,10},{8,4},{10,6},{12,0},{14,2},{1,13},{3,15... | collective-permute-start | bytes 73736 | tf_op jit(solution)/shard_map/ppermute | solution.py:18
  27.9 5.1 %collective-permute-start.9 = (f32[32,128]{1,0:T(8,128)S(1)}, f32[32,128]{1,0:T(8,128)S(1)}, u32[]{:S(2)}, u32[]{:S(2)}) collective-permute-start(f32[32,128]{1,0:T(8,128)S(1)} %pad_maximum_fusion.mine), channel_id=1, source_target_pairs={{0,16},{16,0},{32,48},{48,32},{64,80},{80,64},{96,112},{112,96},{1... | collective-permute-start | bytes 49160 | tf_op jit(solution)/shard_map/ppermute | solution.py:18
  35.1 3.5 %copy-start.1 = (f32[2,1,128]{2,1,0:T(1,128)S(1)}, f32[2,1,128]{2,1,0:T(1,128)}, u32[]{:S(2)}) copy-start(f32[2,1,128]{2,1,0:T(1,128)} %param.13) | copy-start | bytes 3076
  35.1 10.3 %all-to-all-start = ((f32[8,8,128]{2,1,0:T(8,128)}), f32[8,8,128]{2,1,0:T(8,128)S(1)}, u32[]{:S(2)}, u32[]{:S(2)}) async-start(f32[8,8,128]{2,1,0:T(8,128)} %broadcast_in_dim.16), calls=%async_computation | async-start | bytes 65536 | tf_op jit(solution)/shard_map/all_to_all | solution.py:255
  38.6 14.1 %collective-permute-start.10 = (f32[272,128]{1,0:T(8,128)S(1)}, f32[272,128]{1,0:T(8,128)S(1)}, u32[]{:S(2)}, u32[]{:S(2)}) collective-permute-start(f32[272,128]{1,0:T(8,128)S(1)} %second_shear.1.own.cells), channel_id=1, source_target_pairs={{0,32},{16,48},{32,0},{48,16},{64,96},{80,112},{96,64},{112,80},{1... | collective-permute-start | bytes 417800 | tf_op jit(solution)/shard_map/ppermute | solution.py:18
  38.7 14.0 %collective-permute-start.11 = (f32[272,128]{1,0:T(8,128)S(1)}, f32[272,128]{1,0:T(8,128)S(1)}, u32[]{:S(2)}, u32[]{:S(2)}) collective-permute-start(f32[272,128]{1,0:T(8,128)S(1)} %second_shear.1.own.cells), channel_id=1, source_target_pairs={{0,224},{16,240},{32,64},{48,80},{64,32},{80,48},{96,128},{112,144... | collective-permute-start | bytes 417800 | tf_op jit(solution)/shard_map/ppermute | solution.py:18
  46.1 14.2 %all-to-all-start.1 = ((f32[32,8,128]{2,1,0:T(8,128)}), f32[32,8,128]{2,1,0:T(8,128)S(1)}, u32[]{:S(2)}, u32[]{:S(2)}) async-start(f32[32,8,128]{2,1,0:T(8,128)} %broadcast_in_dim.33), calls=%async_computation.1 | async-start | bytes 262144 | tf_op jit(solution)/shard_map/all_to_all | solution.py:255
  53.5 8.2 %collective-permute-start.12 = (f32[128,128]{1,0:T(8,128)S(1)}, f32[128,128]{1,0:T(8,128)S(1)}, u32[]{:S(2)}, u32[]{:S(2)}) collective-permute-start(f32[128,128]{1,0:T(8,128)S(1)} %get-tuple-element.9), channel_id=1, source_target_pairs={{0,16},{16,0},{32,48},{48,32},{64,80},{80,64},{96,112},{112,96},{1... | collective-permute-start | bytes 196616 | tf_op jit(solution)/shard_map/ppermute | solution.py:18
